TPU v7x, 32 devices: a whole 2x2x4 slice. The times are simulated.
32 devices in a mesh: group: 2 (over core), dp: 2 (over x), mp: 8 (over z, y).
Axes of the slice: x: 2, y: 2, z: 4, core: 2. Of those that a mesh axis runs over, the one named last changes fastest.
Arguments:
- latents: float32 [4, 320, 2432], P(('group', 'dp')), may hold values from -6 to 6
- noise: bfloat16 [4, 2, 320, 2432], P(('group', 'dp')), may hold values from -6 to 6
- ref_velocity: bfloat16 [4, 2, 320, 2432], P(('group', 'dp')), may hold values from -6 to 6
- start_step: int32 [4], P(('group', 'dp')), may hold values from 1 to 6
- advantages: float32 [4], P(('group', 'dp')), may hold values from -4 to 4
- behaviour_gap: float32 [4, 2], P(('group', 'dp')), may hold values from -0.4 to 0.4
- modulation: float32 [10, 2, 2432], replicated, may hold values from -3 to 3
- w_in: bfloat16 [2432, 9728], P(('group', 'dp'), 'mp'), may hold values from -6 to 6
- w_down: bfloat16 [2432, 9728], P(('group', 'dp'), 'mp'), may hold values from -6 to 6
Outputs:
- final_latents: float32 [4, 320, 2432], P(('group', 'dp'))
- new_w_in: bfloat16 [2432, 9728], P(('group', 'dp'), 'mp')
- new_w_down: bfloat16 [2432, 9728], P(('group', 'dp'), 'mp')
Inputs may be any that keep to these rules, and one draw needn't show every extreme that they name: `start_step`: the second step of an image is at the next plan position.
All inputs are finite; a program needn't handle non-finite values.
Results may differ from a plain program's by a relative error of at most 0.014.
Values may be sent and summed in bfloat16 or wider, within the bound.
A program may use at most 128 MiB of HBM per device.

v0:
```python
import math

import jax
import jax.numpy as jnp
from jax import lax
from jax.sharding import PartitionSpec as P

SCHED = 10


NOISE_SLOPE = 0.7
CLIP_RANGE = 0.2
GELU_COEF = 0.7978845608028654
GELU_CUBE = 0.044715
HIGH_PREC = lax.Precision.HIGHEST


def gelu_parts(pre_act):
    tangent = jnp.tanh(GELU_COEF * (pre_act + GELU_CUBE * pre_act * pre_act * pre_act))
    activation = 0.5 * pre_act * (1.0 + tangent)
    gelu_slope = 0.5 * (1.0 + tangent) + 0.5 * pre_act * (1.0 - tangent * tangent) * GELU_COEF * (
        1.0 + 3.0 * GELU_CUBE * pre_act * pre_act
    )
    return (activation, gelu_slope)


def on_device(
    latents, noise, ref_velocity, start_step, advantages, behaviour_gap, modulation, w_in, w_down
):
    model_width = latents.shape[2]
    shard_units = w_in.shape[1]
    hidden_width = shard_units * lax.axis_size("mp")
    step_len = 1.0 / SCHED
    vel_coef = 1.0 + 0.5 * NOISE_SLOPE * NOISE_SLOPE
    w_in_full, w_down_full = (
        lax.all_gather(w_in, ("group", "dp"), axis=0, tiled=True),
        lax.all_gather(w_down, ("group", "dp"), axis=0, tiled=True),
    )
    latent_now = latents
    input_list = []
    hidden_list = []
    pre_list = []
    vgrad_list = []
    for step_num in range(2):
        sched_index = start_step + step_num
        time_now = 1.0 - sched_index.astype(jnp.float32) / SCHED
        onehot = (sched_index[:, None] == jnp.arange(SCHED, dtype=jnp.int32)[None, :]).astype(
            jnp.float32
        )
        mod_rows = jnp.einsum("is,scd->icd", onehot, modulation, precision=HIGH_PREC)
        normed = latent_now * lax.rsqrt(
            jnp.mean(latent_now * latent_now, axis=2, keepdims=True) + 1e-06
        )
        inputs = (normed * (1.0 + mod_rows[:, None, 1, :]) + mod_rows[:, None, 0, :]).astype(
            jnp.bfloat16
        )
        pre_act = jnp.einsum(
            "ild,df->ilf", inputs, w_in_full, preferred_element_type=jnp.float32
        ) / math.sqrt(model_width)
        activation, gelu_slope = gelu_parts(pre_act)
        hidden = activation.astype(jnp.bfloat16)
        partial_vel = jnp.einsum(
            "ilf,df->ild", hidden, w_down_full, preferred_element_type=jnp.float32
        ) / math.sqrt(hidden_width)
        velocity = lax.psum(partial_vel.astype(jnp.bfloat16), "mp").astype(jnp.float32)
        noise_level = (NOISE_SLOPE * jnp.sqrt(time_now / (1.0 - time_now)))[:, None, None]
        drift_x = (0.5 * NOISE_SLOPE * NOISE_SLOPE / (1.0 - time_now))[:, None, None]
        eps_draw = noise[:, step_num].astype(jnp.float32)
        ref_vel = ref_velocity[:, step_num].astype(jnp.float32)
        step_mean = latent_now * (1.0 - step_len * drift_x) - step_len * vel_coef * velocity
        latent_now = step_mean + noise_level * math.sqrt(step_len) * eps_draw
        policy_ratio = jnp.exp(behaviour_gap[:, step_num])
        active = (advantages >= 0.0) & (policy_ratio <= 1.0 + CLIP_RANGE) | (advantages < 0.0) & (
            policy_ratio >= 1.0 - CLIP_RANGE
        )
        pg_coef = jnp.where(active, policy_ratio * advantages, jnp.zeros_like(advantages))[
            :, None, None
        ]
        vel_grad = (
            pg_coef * vel_coef * math.sqrt(step_len) * eps_draw / noise_level
            + vel_coef * vel_coef * step_len * (velocity - ref_vel) / (noise_level * noise_level)
        ).astype(jnp.bfloat16)
        hid_grad = jnp.einsum(
            "ild,df->ilf", vel_grad, w_down_full, preferred_element_type=jnp.float32
        ) / math.sqrt(hidden_width)
        pre_list.append((hid_grad * gelu_slope).astype(jnp.bfloat16))
        input_list.append(inputs)
        hidden_list.append(hidden)
        vgrad_list.append(vel_grad)
    inputs_all = jnp.concatenate(input_list, axis=1)
    pre_all = jnp.concatenate(pre_list, axis=1)
    vgrad_all = jnp.concatenate(vgrad_list, axis=1)
    hidden_all = jnp.concatenate(hidden_list, axis=1)
    grad_in = jnp.einsum(
        "ild,ilf->df", inputs_all, pre_all, preferred_element_type=jnp.float32
    ) / math.sqrt(model_width)
    grad_down = jnp.einsum(
        "ild,ilf->df", vgrad_all, hidden_all, preferred_element_type=jnp.float32
    ) / math.sqrt(hidden_width)
    grad_mine = lax.psum_scatter(
        jnp.concatenate([grad_in, grad_down], axis=1).astype(jnp.bfloat16),
        ("group", "dp"),
        scatter_dimension=0,
        tiled=True,
    ).astype(jnp.float32)
    total = lax.psum(jnp.sum(grad_mine * grad_mine), ("group", "dp", "mp"))
    grad_rms = jnp.sqrt(total / (2.0 * model_width * hidden_width) + 1e-06)
    w_both = jnp.concatenate([w_in, w_down], axis=1).astype(jnp.float32)
    new_both = (w_both - grad_mine / grad_rms).astype(jnp.bfloat16)
    return (latent_now, new_both[:, :shard_units], new_both[:, shard_units:])


def solution(mesh):
    return jax.shard_map(
        on_device,
        mesh=mesh,
        in_specs=(
            P(("group", "dp"), None, None),
            P(("group", "dp"), None, None, None),
            P(("group", "dp"), None, None, None),
            P(("group", "dp")),
            P(("group", "dp")),
            P(("group", "dp"), None),
            P(),
            P(("group", "dp"), "mp"),
            P(("group", "dp"), "mp"),
        ),
        out_specs=(
            P(("group", "dp"), None, None),
            P(("group", "dp"), "mp"),
            P(("group", "dp"), "mp"),
        ),
        check_vma=False,
    )
```

profile of v0, /device:TPU:0, one launch (start us, length us, event | category | flops | bytes accessed | tf_op | source)
XLA Modules:
  0.0 516.1 jit_solution(10129704945266284746)
XLA Ops:
  7.2 0.0 all-gather.3.cloned.1.call-start
  7.2 0.7 all-gather.3.cloned.1.call-update
  7.9 0.0 all-gather.5.cloned.1.call-start
  8.0 0.7 all-gather.5.cloned.1.call-update
  8.7 0.0 all-reduce.3.cloned.1.call-start
  9.4 0.2 fusion.55
  9.6 0.1 fusion.62
  9.7 0.3 multiply_reduce_fusion.1
  10.0 1.6 add_convert_fusion.1
  11.6 46.7 %all-gather.3.cloned.1.call-done = bf16[2432,1216]{1,0:T(8,128)(2,1)} async-done(((bf16[608,1216]{1,0:T(8,128)(2,1)}), bf16[2432,1216]{1,0:T(8,128)(2,1)}) %all-gather.3.cloned.1.call-update) | async-done | bytes 5914640 | tf_op jit(solution)/shard_map/all_gather | solution.py:36
  58.3 5.5 %fusion.51 = f32[320,1216]{1,0:T(8,128)S(1)} fusion(bf16[2432,1216]{1,0:T(8,128)(2,1)} %all-gather.3.cloned.1.call-done, bf16[1,320,2432]{2,1,0:T(8,128)(2,1)} %add_convert_fusion.1), kind=kOutput, calls=%fused_computation.80 | convolution fusion | flops 1892679680 | bytes 9027584 | tf_op jit(solution)/shard_map/ild,df->ilf/dot_general | solution.py:57
  63.9 42.1 %all-gather.5.cloned.1.call-done = bf16[2432,1216]{1,0:T(8,128)(2,1)} async-done(((bf16[608,1216]{1,0:T(8,128)(2,1)}), bf16[2432,1216]{1,0:T(8,128)(2,1)}) %all-gather.5.cloned.1.call-update) | async-done | bytes 5914640 | tf_op jit(solution)/shard_map/all_gather | solution.py:37
  105.9 6.3 %fusion.8 = bf16[1,320,2432]{2,1,0:T(8,128)(2,1)} fusion(bf16[2432,1216]{1,0:T(8,128)(2,1)} %all-gather.5.cloned.1.call-done, f32[320,1216]{1,0:T(8,128)S(1)} %fusion.51), kind=kOutput, calls=%fused_computation.23 | convolution fusion | flops 1898127360 | bytes 9027584 | tf_op jit(solution)/shard_map/ilf,df->ild/dot_general | solution.py:62
  112.2 0.0 all-reduce.3.cloned.1.call-update
  112.3 0.0 all-reduce.5.cloned.1.call-start
  112.5 0.2 fusion.53
  112.7 0.1 fusion.59
  112.8 88.5 %all-reduce.3.cloned.1.call-done = bf16[1,320,2432]{2,1,0:T(8,128)(2,1)} async-done(((bf16[1,320,2432]{2,1,0:T(8,128)(2,1)}), bf16[1,320,2432]{2,1,0:T(8,128)(2,1)}) %all-reduce.3.cloned.1.call-update) | async-done | bytes 1556496 | tf_op jit(solution)/shard_map/psum | solution.py:65
  201.3 3.8 multiply_reduce_fusion
  205.1 0.4 add_convert_fusion
  205.6 1.1 copy-done.10
  206.7 5.3 %fusion.49 = f32[320,1216]{1,0:T(8,128)S(1)} fusion(bf16[2432,1216]{1,0:T(8,128)(2,1)} %all-gather.3.cloned.1.call-done, bf16[1,320,2432]{2,1,0:T(8,128)(2,1)S(1)} %add_convert_fusion), kind=kOutput, calls=%fused_computation.78 | convolution fusion | flops 1892679680 | bytes 9027584 | tf_op jit(solution)/shard_map/ild,df->ilf/dot_general | solution.py:57
  212.0 1.2 copy-done.6
  213.2 3.6 fusion.7
  216.8 0.0 all-reduce.5.cloned.1.call-update
  216.8 0.0 reduce-scatter.4.cloned.1.call-start
  217.7 0.7 fusion.77
  219.9 2.9 fusion.73
  222.8 1.5 fusion.74
  224.2 80.9 %all-reduce.5.cloned.1.call-done = bf16[1,320,2432]{2,1,0:T(8,128)(2,1)} async-done(((bf16[1,320,2432]{2,1,0:T(8,128)(2,1)}), bf16[1,320,2432]{2,1,0:T(8,128)(2,1)}) %all-reduce.5.cloned.1.call-update) | async-done | bytes 1556496 | tf_op jit(solution)/shard_map/psum | solution.py:65
  305.2 6.3 %fusion.30 = (bf16[1,320,2432]{2,1,0:T(8,128)(2,1)S(1)}, bf16[1,320,2432]{2,1,0:T(8,128)(2,1)S(1)}, f32[1,320,2432]{2,1,0:T(8,128)}) fusion(bf16[1,320,2432]{2,1,0:T(8,128)(2,1)} %all-reduce.3.cloned.1.call-done, f32[]{:T(128)} %bitcast.22, bf16[1,2,320,2432]{3,2,1,0:T(8,128)(2,1)} %param.11, f32[]{:T(128)} %bitcast.19, f32[]{:T(128)} %bitcast.18, ...), kind=kLoop, calls=%fused_computation.51 | loop fusion | flops 19456000 | bytes 18677792 | tf_op jit(solution)/shard_map/convert_element_type | solution.py:82
  311.6 5.4 %fusion.1 = bf16[2432,1216]{0,1:T(8,128)(2,1)S(1)} fusion(bf16[1,320,2432]{2,1,0:T(8,128)(2,1)S(1)} %get-tuple-element.16, bf16[1,320,2432]{2,1,0:T(8,128)(2,1)S(1)} %get-tuple-element.15, bf16[1,320,1216]{2,1,0:T(8,128)(2,1)S(1)} %copy-done.13, bf16[1,320,1216]{2,1,0:T(8,128)(2,1)S(1)} %copy-done.12), kind=kOutput, calls=%fused_computation.4 | convolution fusion | flops 3800612864 | bytes 10584064 | tf_op jit(solution)/shard_map/ild,ilf->df/dot_general | solution.py:97
  317.0 2.9 fusion.36
  319.9 2.9 fusion.35
  322.9 5.4 %fusion = bf16[2432,1216]{0,1:T(8,128)(2,1)S(1)} fusion(bf16[1,320,2432]{2,1,0:T(8,128)(2,1)S(1)} %copy-done.11, bf16[1,320,2432]{2,1,0:T(8,128)(2,1)S(1)} %copy-done.9, bf16[1,320,1216]{2,1,0:T(8,128)(2,1)S(1)} %fusion.36, bf16[1,320,1216]{2,1,0:T(8,128)(2,1)S(1)} %fusion.35), kind=kOutput, calls=%fused_computation.3 | convolution fusion | flops 3800612864 | bytes 10584064 | tf_op jit(solution)/shard_map/ild,ilf->df/dot_general | solution.py:94
  328.3 13.2 %pad_maximum_fusion = bf16[2432,2432]{0,1:T(8,128)(2,1)} fusion(bf16[2432,1216]{0,1:T(8,128)(2,1)S(1)} %fusion.1, bf16[2432,1216]{0,1:T(8,128)(2,1)S(1)} %fusion), kind=kLoop, calls=%fused_computation.2 | loop fusion | flops 23658496 | bytes 23658496 | tf_op jit(solution)/shard_map/concatenate | solution.py:101
  341.5 16.7 %copy.23 = bf16[2432,2432]{1,0:T(8,128)(2,1)} copy(bf16[2432,2432]{0,1:T(8,128)(2,1)} %pad_maximum_fusion) | data formatting | bytes 23658496
  358.2 1.4 copy-done.3
  359.6 2.2 copy.17
  361.8 90.1 %reduce-scatter.4.cloned.1.call-done = bf16[608,2432]{1,0:T(8,128)(2,1)} async-done(((bf16[2432,2432]{1,0:T(8,128)(2,1)}), bf16[608,2432]{1,0:T(8,128)(2,1)}) %reduce-scatter.4.cloned.1.call-update) | async-done | bytes 2957328
  451.8 4.2 copy.24
  456.0 2.3 fusion.2
  458.3 3.5 copy.16
  461.7 39.5 %psum.23 = f32[]{:T(128)} all-reduce(f32[]{:T(128)} %fusion.2), channel_id=1, replica_groups=mesh['group'=2,'dp'=2,'mp'=8] {'group','dp','mp'}, use_global_device_ids=true, to_apply=%region_6.7 | all-reduce | flops 1 | bytes 8 | tf_op jit(solution)/shard_map/psum | solution.py:106
  501.9 2.9 fusion.4
  504.9 0.3 fusion.76
  505.1 2.2 copy.18
  507.4 2.2 copy.19
  (40 shorter events, 0.1 us)
Async XLA Ops:
  7.2 2.2 copy-start
  7.2 2.5 copy-start.2
  7.2 51.1 %all-gather.3.cloned.1.call-start = ((), (), s32[]{:S(2)}) async-start(), calls=%async_computation.1 | async-start | bytes 7782400 | tf_op jit(solution)/shard_map/all_gather | solution.py:36
  7.9 98.0 %all-gather.5.cloned.1.call-start = ((), (), s32[]{:S(2)}) async-start(), calls=%async_computation.2 | async-start | bytes 7782400 | tf_op jit(solution)/shard_map/all_gather | solution.py:37
  8.7 192.6 %all-reduce.3.cloned.1.call-start = ((), (), s32[]{:S(2)}) async-start(), calls=%async_computation.3 | async-start | bytes 3112960 | tf_op jit(solution)/shard_map/psum | solution.py:65
  63.9 48.4 %copy-start.4 = (f32[320,1216]{1,0:T(8,128)}, f32[320,1216]{1,0:T(8,128)S(1)}, u32[]{:S(2)}) copy-start(f32[320,1216]{1,0:T(8,128)S(1)} %fusion.51) | copy-start | bytes 4669444
  112.3 192.9 %all-reduce.5.cloned.1.call-start = ((), (), s32[]{:S(2)}) async-start(), calls=%async_computation.4 | async-start | bytes 3112960 | tf_op jit(solution)/shard_map/psum | solution.py:65
  205.1 8.1 %slice-start = ((s8[6225920]{0:T(1024)(128)(4,1)}), s8[4194304]{0:T(1024)(128)(4,1)S(1)}, s32[]{:S(2)}) async-start(s8[6225920]{0:T(1024)(128)(4,1)} %bitcast.113), calls=%async_computation.6 | async-start | bytes 8388608
  205.5 1.2 copy-start.10
  206.7 6.5 %slice-start.1 = ((s8[6225920]{0:T(1024)(128)(4,1)}), s8[2031616]{0:T(1024)(128)(4,1)S(1)}, s32[]{:S(2)}) async-start(s8[6225920]{0:T(1024)(128)(4,1)} %bitcast.113), calls=%async_computation.7 | async-start | bytes 4063232
  212.0 1.2 copy-start.6
  213.2 4.6 copy-start.14
  216.8 235.0 %reduce-scatter.4.cloned.1.call-start = ((), (), s32[]{:S(2)}) async-start(), calls=%async_computation.5 | async-start | bytes 14786560
  216.9 5.9 %copy-start.7 = (f32[320,1216]{1,0:T(8,128)S(1)}, f32[320,1216]{1,0:T(8,128)}, u32[]{:S(2)}) copy-start(f32[320,1216]{1,0:T(8,128)} %copy-done.6) | copy-start | bytes 4669444
  305.2 6.3 %copy-start.12 = (bf16[1,320,1216]{2,1,0:T(8,128)(2,1)S(1)}, bf16[1,320,1216]{2,1,0:T(8,128)(2,1)}, u32[]{:S(2)}) copy-start(bf16[1,320,1216]{2,1,0:T(8,128)(2,1)} %fusion.73) | copy-start | bytes 2334724
  305.2 6.3 %copy-start.13 = (bf16[1,320,1216]{2,1,0:T(8,128)(2,1)S(1)}, bf16[1,320,1216]{2,1,0:T(8,128)(2,1)}, u32[]{:S(2)}) copy-start(bf16[1,320,1216]{2,1,0:T(8,128)(2,1)} %fusion.74) | copy-start | bytes 2334724
  305.2 11.8 %slice-start.2 = ((s8[6225920]{0:T(1024)(128)(4,1)}), s8[4194304]{0:T(1024)(128)(4,1)S(1)}, s32[]{:S(2)}) async-start(s8[6225920]{0:T(1024)(128)(4,1)} %bitcast.115), calls=%async_computation.8 | async-start | bytes 8388608
  311.5 5.5 %copy-start.8 = (f32[320,1216]{1,0:T(8,128)S(1)}, f32[320,1216]{1,0:T(8,128)}, u32[]{:S(2)}) copy-start(f32[320,1216]{1,0:T(8,128)} %copy-done.6) | copy-start | bytes 4669444
  311.5 5.5 %slice-start.3 = ((s8[6225920]{0:T(1024)(128)(4,1)}), s8[2031616]{0:T(1024)(128)(4,1)S(1)}, s32[]{:S(2)}) async-start(s8[6225920]{0:T(1024)(128)(4,1)} %bitcast.115), calls=%async_computation.9 | async-start | bytes 4063232
  317.0 2.9 copy-start.5
  319.9 2.9 copy-start.9
  319.9 2.9 copy-start.11
  358.2 1.4 copy-start.3
  505.1 4.4 copy-start.1
Sparse Core Ops, SparseCore 0:
  9.6 48.6 all-gather.2
  59.9 45.9 all-gather.4
  112.4 88.8 all-reduce.2
  216.9 88.2 all-reduce.4
  358.3 93.4 reduce-scatter.3
where the time goes:
time: 517 us; the launch traced here: 516 us
  waiting for transfers between devices  350 us (68%)
  blocking collectives  39.5 us (8%)
  matrix products  37.8 us (7%)
  local copies, waits for them, and re-layouts  35.6 us (7%)
  other arithmetic  35.4 us (7%)
  between operations  17.9 us (3%)
    psum x2, waiting for transfers between devices, on_device(): lax.psum(partial_vel.astype(jnp.bfloat16), 'mp').astype(jnp.float32)  169 us
    unnamed x6, waiting for transfers between devices  91.5 us
    all_gather x1, waiting for transfers between devices, on_device(): lax.all_gather(w_in, ('group', 'dp'), axis=0, tiled=True)  46.7 us
    all_gather x1, waiting for transfers between devices, on_device(): lax.all_gather(w_down, ('group', 'dp'), axis=0, tiled=True)  42.1 us
    psum x1, blocking collectives, on_device(): total = lax.psum(jnp.sum(grad_mine * grad_mine), ('group', 'dp', 'mp'))  39.5 us
    unnamed x44, local copies, waits for them, and re-layouts  34.7 us
    concatenate x1, other arithmetic, on_device(): jnp.concatenate([grad_in, grad_down], axis=1).astype(jnp.bfloat16)  13.2 us
    dot_general x2, matrix products, on_device(): jnp.einsum('ild,df->ilf', inputs, w_in_full, preferred_element_type=jnp.f...  10.8 us
  transfers between devices with their start and end apart: 5, of which 5 were waited for; matrix products, arithmetic and copies ran while one was open for 3% of the time, Pallas kernels for 0%

commit v1 on v0

--- a/solution.py
+++ b/solution.py
@@ -1,8 +1,11 @@
+import functools
 import math
 
 import jax
 import jax.numpy as jnp
 from jax import lax
+from jax.experimental import pallas as pl
+from jax.experimental.pallas import tpu as pltpu
 from jax.sharding import PartitionSpec as P
 
 SCHED = 10
@@ -13,6 +16,310 @@
 GELU_COEF = 0.7978845608028654
 GELU_CUBE = 0.044715
 HIGH_PREC = lax.Precision.HIGHEST
+MESH = pl.DeviceIdType.MESH
+F32 = jnp.float32
+BF16 = jnp.bfloat16
+VMEM_LIMIT = 56 * 1024 * 1024
+
+
+def params(collective_id):
+    return pltpu.CompilerParams(
+        collective_id=collective_id, has_side_effects=True, vmem_limit_bytes=VMEM_LIMIT
+    )
+
+
+def remote(src, dst, send_sem, recv_sem, **axes):
+    return pltpu.make_async_remote_copy(
+        src_ref=src, dst_ref=dst, send_sem=send_sem, recv_sem=recv_sem,
+        device_id=axes, device_id_type=MESH,
+    )
+
+
+def greet(peers):
+    barrier = pltpu.get_barrier_semaphore()
+    for axes in peers:
+        pl.semaphore_signal(barrier, inc=1, device_id=axes, device_id_type=MESH)
+    pl.semaphore_wait(barrier, len(peers))
+
+
+def row_chunks(rows):
+    parts = 2 if rows % 32 == 0 else 1
+    size = rows // parts
+    return [pl.ds(c * size, size) for c in range(parts)]
+
+
+def gather_kernel(nd, w_in, w_down, out_in, out_down, xs, xr, fs, fr, os, orr, ls):
+    g, d = lax.axis_index("group"), lax.axis_index("dp")
+    other = 1 - g
+    targets = [lax.rem(d + o, nd) for o in range(nd)]
+    sources = [lax.rem(d - o + nd, nd) for o in range(nd)]
+    greet([{"group": other}] + [{"dp": targets[o]} for o in range(1, nd)])
+    chunks = row_chunks(w_in.shape[0])
+    mine = g * nd + d
+    pairs = ((w_in, out_in), (w_down, out_down))
+    pending = []
+    for a, (src, dst) in enumerate(pairs):
+        for c, rows in enumerate(chunks):
+            for o in range(1, nd):
+                copy = remote(src.at[rows], dst.at[mine, rows], xs.at[a, c, o], xr.at[a, c, o], dp=targets[o])
+                copy.start()
+                pending.append(copy)
+    local = []
+    for a, (src, dst) in enumerate(pairs):
+        copy = remote(src, dst.at[mine], os.at[a], orr.at[a], group=other)
+        copy.start()
+        pending.append(copy)
+        keep = pltpu.make_async_copy(src, dst.at[mine], ls.at[a])
+        keep.start()
+        local.append(keep)
+    for a, (src, dst) in enumerate(pairs):
+        for c, rows in enumerate(chunks):
+            for o in range(1, nd):
+                block = g * nd + sources[o]
+                remote(src.at[rows], dst.at[block, rows], xs.at[a, c, o], xr.at[a, c, o], dp=targets[o]).wait_recv()
+                copy = remote(dst.at[block, rows], dst.at[block, rows], fs.at[a, c, o], fr.at[a, c, o], group=other)
+                copy.start()
+                pending.append(copy)
+    for a, (src, dst) in enumerate(pairs):
+        remote(src, dst.at[other * nd + d], os.at[a], orr.at[a], group=other).wait_recv()
+        for c, rows in enumerate(chunks):
+            for o in range(1, nd):
+                block = other * nd + sources[o]
+                remote(dst.at[block, rows], dst.at[block, rows], fs.at[a, c, o], fr.at[a, c, o], group=other).wait_recv()
+    for copy in pending:
+        copy.wait_send()
+    for copy in local:
+        copy.wait()
+
+
+def gather_weights(w_in, w_down, ng, nd):
+    rows, units = w_in.shape
+    nc = len(row_chunks(rows))
+    dma = pltpu.SemaphoreType.DMA
+    shape = jax.ShapeDtypeStruct((ng * nd, rows, units), w_in.dtype)
+    full_in, full_down = pl.pallas_call(
+        functools.partial(gather_kernel, nd),
+        out_shape=(shape, shape),
+        in_specs=[pl.BlockSpec(memory_space=pl.ANY)] * 2,
+        out_specs=(pl.BlockSpec(memory_space=pl.ANY),) * 2,
+        scratch_shapes=[
+            dma((2, nc, nd)), dma((2, nc, nd)), dma((2, nc, nd)), dma((2, nc, nd)),
+            dma((2,)), dma((2,)), dma((2,)),
+        ],
+        compiler_params=params(1),
+        name="gather_weights",
+    )(w_in, w_down)
+    return full_in.reshape(ng * nd * rows, units), full_down.reshape(ng * nd * rows, units)
+
+
+def sum_kernel(no, src, out, ybuf, zsum, zbuf, ys, yr, zs, zr, gzs, gzr, gys, gyr):
+    m = lax.axis_index("mp")
+    y, z = lax.rem(m, 2), lax.div(m, 2)
+    partner = z * 2 + 1 - y
+    ahead = [lax.rem(z + o, no) for o in range(no)]
+    behind = [lax.rem(z - o + no, no) for o in range(no)]
+    greet([{"mp": partner}] + [{"mp": ahead[o] * 2 + y} for o in range(1, no)])
+    order = list(range(1, no)) + [0]
+    pending = []
+    for o in order:
+        copy = remote(src.at[ahead[o] * 2 + 1 - y], ybuf.at[o], ys.at[o], yr.at[o], mp=partner)
+        copy.start()
+        pending.append(copy)
+    for o in order[:-1]:
+        remote(src.at[ahead[o] * 2 + 1 - y], ybuf.at[o], ys.at[o], yr.at[o], mp=partner).wait_recv()
+        zsum[o] = (src[ahead[o] * 2 + y].astype(F32) + ybuf[o].astype(F32)).astype(BF16)
+        copy = remote(zsum.at[o], zbuf.at[o], zs.at[o], zr.at[o], mp=ahead[o] * 2 + y)
+        copy.start()
+        pending.append(copy)
+    remote(src.at[z * 2 + 1 - y], ybuf.at[0], ys.at[0], yr.at[0], mp=partner).wait_recv()
+    total = src[m].astype(F32) + ybuf[0].astype(F32)
+    for o in range(1, no):
+        remote(zsum.at[o], zbuf.at[o], zs.at[o], zr.at[o], mp=ahead[o] * 2 + y).wait_recv()
+        total = total + zbuf[o].astype(F32)
+    out[m] = total.astype(BF16)
+    for o in range(1, no):
+        copy = remote(out.at[m], out.at[m], gzs.at[o], gzr.at[o], mp=ahead[o] * 2 + y)
+        copy.start()
+        pending.append(copy)
+    copy = remote(out.at[m], out.at[m], gys.at[0], gyr.at[0], mp=partner)
+    copy.start()
+    pending.append(copy)
+    for o in range(1, no):
+        block = out.at[behind[o] * 2 + y]
+        remote(block, block, gzs.at[o], gzr.at[o], mp=ahead[o] * 2 + y).wait_recv()
+        copy = remote(block, block, gys.at[o], gyr.at[o], mp=partner)
+        copy.start()
+        pending.append(copy)
+    for o in range(no):
+        block = out.at[behind[o] * 2 + 1 - y]
+        remote(block, block, gys.at[o], gyr.at[o], mp=partner).wait_recv()
+    for copy in pending:
+        copy.wait_send()
+
+
+def sum_over_mp(part, n, collective_id):
+    images, tokens, width = part.shape
+    no, rows = n // 2, images * tokens // n
+    dma = pltpu.SemaphoreType.DMA
+    vmem = pl.BlockSpec(memory_space=pltpu.VMEM)
+    summed = pl.pallas_call(
+        functools.partial(sum_kernel, no),
+        out_shape=jax.ShapeDtypeStruct((n, rows, width), BF16),
+        in_specs=[vmem],
+        out_specs=vmem,
+        scratch_shapes=[pltpu.VMEM((no, rows, width), BF16)] * 3 + [dma((no,))] * 8,
+        compiler_params=params(collective_id),
+        name="sum_over_mp",
+    )(part.reshape(n, rows, width))
+    return summed.reshape(images, tokens, width)
+
+
+def update_kernel(
+    nd, n, count, g_in, g_down, w_in, w_down, new_in, new_down,
+    own, sib, far, total, sq_mp, sq_gd, cs, cr, xs, xr, ls, ms, mr, ps, pr,
+):
+    g, d, m = lax.axis_index("group"), lax.axis_index("dp"), lax.axis_index("mp")
+    other = 1 - g
+    targets = [lax.rem(d + o, nd) for o in range(nd)]
+    mp_peers = [lax.rem(m + o, n) for o in range(n)]
+    gd_peers = [(h, o) for h in range(2) for o in range(nd)]
+    place = lambda h: g if h == 0 else other
+    greet(
+        [{"group": place(h), "dp": targets[o]} for h, o in gd_peers[1:]]
+        + [{"mp": mp_peers[o]} for o in range(1, n)]
+    )
+    rows = w_in.shape[0]
+    chunks = row_chunks(rows)
+    order = list(range(1, nd)) + [0]
+    grads = (g_in, g_down)
+    pending = []
+    loads = {}
+    for o in order:
+        for a in range(2):
+            for c, part in enumerate(chunks):
+                copy = remote(
+                    grads[a].at[other * nd + targets[o], part], sib.at[a, o, part],
+                    cs.at[a, o, c], cr.at[a, o, c], group=other,
+                )
+                copy.start()
+                pending.append(copy)
+                load = pltpu.make_async_copy(
+                    grads[a].at[g * nd + targets[o], part], own.at[a, o, part], ls.at[a, o, c]
+                )
+                load.start()
+                loads[a, o, c] = (load, copy)
+    step = 16
+    def tiles(part, body, init):
+        return lax.fori_loop(0, part.size // step, lambda i, v: body(pl.ds(pl.multiple_of(part.start + i * step, step), step), v), init)
+    for o in order[:-1]:
+        for a in range(2):
+            for c, part in enumerate(chunks):
+                load, copy = loads[a, o, c]
+                load.wait()
+                copy.wait_recv()
+                def add(at, _):
+                    sib[a, o, at] = (sib[a, o, at].astype(F32) + own[a, o, at].astype(F32)).astype(BF16)
+                    return 0
+                tiles(part, add, 0)
+                send = remote(sib.at[a, o, part], far.at[a, o - 1, part], xs.at[a, o, c], xr.at[a, o, c], dp=targets[o])
+                send.start()
+                pending.append(send)
+                loads[a, o, c] = send
+    square = jnp.zeros((step, w_in.shape[1]), F32)
+    for a in range(2):
+        for c, part in enumerate(chunks):
+            load, copy = loads[a, 0, c]
+            load.wait()
+            copy.wait_recv()
+            def near(at, _):
+                total[a, at] = sib[a, 0, at].astype(F32) + own[a, 0, at].astype(F32)
+                return 0
+            tiles(part, near, 0)
+    for a in range(2):
+        for c, part in enumerate(chunks):
+            for o in order[:-1]:
+                loads[a, o, c].wait_recv()
+            def finish(at, sq):
+                value = total[a, at]
+                for o in order[:-1]:
+                    value = value + far[a, o - 1, at].astype(F32)
+                total[a, at] = value
+                return sq + value * value
+            square = tiles(part, finish, square)
+    sq_mp[0] = jnp.full((8, 128), jnp.sum(square), F32)
+    sends = []
+    for o in range(1, n):
+        copy = remote(sq_mp.at[0], sq_mp.at[o], ms.at[o], mr.at[o], mp=mp_peers[o])
+        copy.start()
+        sends.append(copy)
+    for copy in sends:
+        copy.wait_recv()
+    pending += sends
+    value = sq_mp[0]
+    for o in range(1, n):
+        value = value + sq_mp[o]
+    sq_gd[0] = value
+    sends = []
+    for p, (h, o) in enumerate(gd_peers):
+        if p:
+            copy = remote(sq_gd.at[0], sq_gd.at[p], ps.at[p], pr.at[p], group=place(h), dp=targets[o])
+            copy.start()
+            sends.append(copy)
+    for copy in sends:
+        copy.wait_recv()
+    pending += sends
+    for p in range(1, len(gd_peers)):
+        value = value + sq_gd[p]
+    inverse = lax.rsqrt(value[0:1, 0:1] / count + 1e-06)
+    for a, (w, new) in enumerate(((w_in, new_in), (w_down, new_down))):
+        def update(at, _):
+            new[at] = (w[at].astype(F32) - total[a, at] * inverse).astype(BF16)
+            return 0
+        tiles(pl.ds(0, rows), update, 0)
+    for copy in pending:
+        copy.wait_send()
+
+
+def update_weights(grad_in, grad_down, w_in, w_down, ng, nd, n):
+    rows, units = w_in.shape
+    nc = len(row_chunks(rows))
+    count = 2.0 * rows * ng * nd * units * n
+    dma = pltpu.SemaphoreType.DMA
+    vmem = pl.BlockSpec(memory_space=pltpu.VMEM)
+    hbm = pl.BlockSpec(memory_space=pl.ANY)
+    shape = jax.ShapeDtypeStruct((rows, units), w_in.dtype)
+    return pl.pallas_call(
+        functools.partial(update_kernel, nd, n, count),
+        out_shape=(shape, shape),
+        in_specs=[hbm, hbm, vmem, vmem],
+        out_specs=(vmem, vmem),
+        scratch_shapes=[
+            pltpu.VMEM((2, nd, rows, units), BF16),
+            pltpu.VMEM((2, nd, rows, units), BF16),
+            pltpu.VMEM((2, nd - 1, rows, units), BF16),
+            pltpu.VMEM((2, rows, units), F32),
+            pltpu.VMEM((n, 8, 128), F32),
+            pltpu.VMEM((ng * nd, 8, 128), F32),
+            dma((2, nd, nc)), dma((2, nd, nc)), dma((2, nd, nc)), dma((2, nd, nc)), dma((2, nd, nc)),
+            dma((n,)), dma((n,)), dma((ng * nd,)), dma((ng * nd,)),
+        ],
+        compiler_params=params(4),
+        name="update_weights",
+    )(grad_in.reshape(ng * nd, rows, units), grad_down.reshape(ng * nd, rows, units), w_in, w_down)
+
+
+def update_by_ops(grad_in, grad_down, w_in, w_down, ng, nd, n):
+    rows, units = w_in.shape
+    count = 2.0 * rows * ng * nd * units * n
+    mine = [
+        lax.psum_scatter(grad, ("group", "dp"), scatter_dimension=0, tiled=True).astype(F32)
+        for grad in (grad_in, grad_down)
+    ]
+    total = lax.psum(sum(jnp.sum(grad * grad) for grad in mine), ("group", "dp", "mp"))
+    rms = jnp.sqrt(total / count + 1e-06)
+    return tuple(
+        (w.astype(F32) - grad / rms).astype(BF16) for w, grad in zip((w_in, w_down), mine)
+    )
 
 
 def gelu_parts(pre_act):
@@ -29,13 +336,11 @@
 ):
     model_width = latents.shape[2]
     shard_units = w_in.shape[1]
-    hidden_width = shard_units * lax.axis_size("mp")
+    ng, nd, n = lax.axis_size("group"), lax.axis_size("dp"), lax.axis_size("mp")
+    hidden_width = shard_units * n
     step_len = 1.0 / SCHED
     vel_coef = 1.0 + 0.5 * NOISE_SLOPE * NOISE_SLOPE
-    w_in_full, w_down_full = (
-        lax.all_gather(w_in, ("group", "dp"), axis=0, tiled=True),
-        lax.all_gather(w_down, ("group", "dp"), axis=0, tiled=True),
-    )
+    w_in_full, w_down_full = gather_weights(w_in, w_down, ng, nd)
     latent_now = latents
     input_list = []
     hidden_list = []
@@ -62,7 +367,7 @@
         partial_vel = jnp.einsum(
             "ilf,df->ild", hidden, w_down_full, preferred_element_type=jnp.float32
         ) / math.sqrt(hidden_width)
-        velocity = lax.psum(partial_vel.astype(jnp.bfloat16), "mp").astype(jnp.float32)
+        velocity = sum_over_mp(partial_vel.astype(BF16), n, 2 + step_num).astype(jnp.float32)
         noise_level = (NOISE_SLOPE * jnp.sqrt(time_now / (1.0 - time_now)))[:, None, None]
         drift_x = (0.5 * NOISE_SLOPE * NOISE_SLOPE / (1.0 - time_now))[:, None, None]
         eps_draw = noise[:, step_num].astype(jnp.float32)
@@ -97,17 +402,10 @@
     grad_down = jnp.einsum(
         "ild,ilf->df", vgrad_all, hidden_all, preferred_element_type=jnp.float32
     ) / math.sqrt(hidden_width)
-    grad_mine = lax.psum_scatter(
-        jnp.concatenate([grad_in, grad_down], axis=1).astype(jnp.bfloat16),
-        ("group", "dp"),
-        scatter_dimension=0,
-        tiled=True,
-    ).astype(jnp.float32)
-    total = lax.psum(jnp.sum(grad_mine * grad_mine), ("group", "dp", "mp"))
-    grad_rms = jnp.sqrt(total / (2.0 * model_width * hidden_width) + 1e-06)
-    w_both = jnp.concatenate([w_in, w_down], axis=1).astype(jnp.float32)
-    new_both = (w_both - grad_mine / grad_rms).astype(jnp.bfloat16)
-    return (latent_now, new_both[:, :shard_units], new_both[:, shard_units:])
+    held = 6 * nd * w_in.size * 2 + 4 * w_in.size * 4
+    update = update_weights if held < VMEM_LIMIT * 3 // 4 else update_by_ops
+    new_in, new_down = update(grad_in.astype(BF16), grad_down.astype(BF16), w_in, w_down, ng, nd, n)
+    return (latent_now, new_in, new_down)
 
 
 def solution(mesh):

time: 517 us -> 389 us (0.75)
  waiting for transfers between devices: 350 us -> 0 us
  Pallas kernels: 0 us -> 298 us
  blocking collectives: 39.5 us -> 0 us
  other arithmetic: 35.4 us -> 13.8 us
  between operations: 17.9 us -> 3.93 us
  local copies, waits for them, and re-layouts: 35.6 us -> 26.5 us
  matrix products: 37.8 us -> 45.8 us
    pallas_call x0 -> x4, Pallas kernels: none -> 298 us  [the longest x2 107 us: sum_over_mp(): pl.pallas_call(functools.partial(sum_kernel, no), out_shape=jax.ShapeDtyp...]
    psum x2 -> x0, waiting for transfers between devices: 169 us -> none  [on_device(): lax.psum(partial_vel.astype(jnp.bfloat16), 'mp').astype(jnp.float32)]
    unnamed x6 -> x0, waiting for transfers between devices: 91.5 us -> none
    all_gather x2 -> x0, waiting for transfers between devices: 88.8 us -> none  [the longest x1 46.7 us: on_device(): lax.all_gather(w_in, ('group', 'dp'), axis=0, tiled=True)]
    psum x1 -> x0, blocking collectives: 39.5 us -> none  [on_device(): total = lax.psum(jnp.sum(grad_mine * grad_mine), ('group', 'dp', 'mp'))]
    unnamed x44, local copies, waits for them, and re-layouts: 34.7 us -> 6.32 us
    convert_element_type x0 -> x2, local copies, waits for them, and re-layouts: none -> 18.9 us  [the longest x1 9.52 us: on_device(): grad_down.astype(BF16)]
    concatenate x1 -> x0, other arithmetic: 13.2 us -> none  [on_device(): jnp.concatenate([grad_in, grad_down], axis=1).astype(jnp.bfloat16)]
  transfers between devices with their start and end apart: 5 -> 0, of which waited for: 5 -> 0; matrix products, arithmetic and copies ran while one was open for 3% -> 0% of each run, Pallas kernels for 0% -> 0%
where the time goes in v1:
time: 389 us; the launch traced here: 388 us
  Pallas kernels  298 us (77%)
  matrix products  45.8 us (12%)
  local copies, waits for them, and re-layouts  26.5 us (7%)
  other arithmetic  13.8 us (4%)
  between operations  3.93 us (1%)
    pallas_call x2, Pallas kernels, sum_over_mp(): pl.pallas_call(functools.partial(sum_kernel, no), out_shape=jax.ShapeDtyp...  107 us
    pallas_call x1, Pallas kernels, gather_weights(): pl.pallas_call(functools.partial(gather_kernel, nd), out_shape=(shape, sh...  98.7 us
    pallas_call x1, Pallas kernels, update_weights(): pl.pallas_call(functools.partial(update_kernel, nd, n, count), out_shape=...  92.3 us
    dot_general x2, matrix products, on_device(): jnp.einsum('ild,df->ilf', vel_grad, w_down_full, preferred_element_type=j...  15.1 us
    convert_element_type x1, local copies, waits for them, and re-layouts, on_device(): grad_down.astype(BF16)  9.52 us
    convert_element_type x1, local copies, waits for them, and re-layouts, on_device(): grad_in.astype(BF16)  9.39 us
    dot_general x1, matrix products, on_device(): jnp.einsum('ild,ilf->df', inputs_all, pre_all, preferred_element_type=jnp...  8.41 us

profile of v1, /device:TPU:0, one launch (start us, length us, event | category | flops | bytes accessed | tf_op | source)
XLA Modules:
  0.0 388.5 jit_solution(2429645964477587487)
XLA Ops:
  0.6 0.0 copy-start
  2.2 1.3 fusion.93
  5.0 0.0 copy-start.2
  5.0 2.3 multiply_reduce_fusion.1
  7.3 0.0 copy-done
  7.3 0.2 fusion.68
  7.6 0.1 fusion.74
  7.6 0.2 fusion.70
  7.9 0.1 fusion.77
  7.9 0.0 copy-done.2
  7.9 0.4 add_convert_fusion.1
  8.4 98.7 %gather_weights.1 = (bf16[4,608,1216]{2,1,0:T(8,128)(2,1)}, bf16[4,608,1216]{2,1,0:T(8,128)(2,1)}) custom-call(bf16[608,1216]{1,0:T(8,128)(2,1)} %w_in.3, bf16[608,1216]{1,0:T(8,128)(2,1)} %w_down.3), custom_call_target="tpu_custom_call" | custom-call | tf_op jit(solution)/shard_map/gather_weights/pallas_call | solution.py:100
  107.1 0.0 copy-start.16
  107.1 5.2 %fusion.54 = f32[320,1216]{1,0:T(8,128)S(1)} fusion(bf16[2432,1216]{1,0:T(8,128)(2,1)} %bitcast.165, bf16[1,320,2432]{2,1,0:T(8,128)(2,1)S(1)} %add_convert_fusion.1), kind=kOutput, calls=%fused_computation.82 | convolution fusion | flops 1892679680 | bytes 9027584 | tf_op jit(solution)/shard_map/ild,df->ilf/dot_general | solution.py:362
  112.3 3.6 fusion.2
  115.9 53.1 %sum_over_mp.2 = bf16[8,40,2432]{2,1,0:T(8,128)(2,1)} custom-call(bf16[8,40,2432]{2,1,0:T(8,128)(2,1)} %bitcast.157), custom_call_target="tpu_custom_call" | custom-call | tf_op jit(solution)/shard_map/sum_over_mp/pallas_call | solution.py:165
  169.0 0.0 copy-start.5
  169.1 0.0 slice-start.2
  169.1 1.8 convert_element_type.258
  170.8 0.6 copy-done.5
  171.4 7.8 %fusion.38 = bf16[1,320,1216]{2,1,0:T(8,128)(2,1)} fusion(bf16[2432,1216]{1,0:T(8,128)(2,1)} %bitcast.159, f32[320,1216]{1,0:T(8,128)S(1)} %fusion.54, f32[1,1,320,2432]{3,2,1,0:T(8,128)S(1)} %bitcast.150, f32[]{:T(128)} %bitcast.25, f32[]{:T(128)} %bitcast.23, f32[]{:T(128)} %bitcast.22, bf16[1,2,320,2432]{3,2,1,0:T(8,128)(2,1)} %param.11, ...), kind=kOutput, calls=%fused_computation.60 | convolution fusion | flops 1907855360 | bytes 14870016 | tf_op jit(solution)/shard_map/ild,df->ilf/dot_general | solution.py:388
  179.2 1.0 multiply_reduce_fusion
  180.2 0.0 slice-start
  180.2 0.4 add_convert_fusion
  180.7 1.2 copy-done.3
  181.9 0.0 slice-done.2
  181.9 0.0 slice-start.1
  181.9 2.3 fusion.52
  184.2 2.5 fusion.90
  186.7 0.0 slice-done
  186.7 3.6 fusion.3
  190.3 54.3 %sum_over_mp.3 = bf16[8,40,2432]{2,1,0:T(8,128)(2,1)} custom-call(bf16[8,40,2432]{2,1,0:T(8,128)(2,1)} %bitcast.158), custom_call_target="tpu_custom_call" | custom-call | tf_op jit(solution)/shard_map/sum_over_mp/pallas_call | solution.py:165
  244.6 0.0 copy-start.6
  244.7 1.8 convert_element_type.259
  246.4 0.6 copy-done.6
  247.0 7.4 %fusion.39 = bf16[1,320,1216]{2,1,0:T(8,128)(2,1)} fusion(bf16[2432,1216]{1,0:T(8,128)(2,1)} %bitcast.160, f32[320,1216]{1,0:T(8,128)} %copy-done.8, f32[1,1,320,2432]{3,2,1,0:T(8,128)S(1)} %bitcast.155, f32[]{:T(128)} %bitcast.32, f32[]{:T(128)} %bitcast.30, f32[]{:T(128)} %bitcast.29, bf16[1,2,320,2432]{3,2,1,0:T(8,128)(2,1)S(1)} %copy-done.7, ...), kind=kOutput, calls=%fused_computation.61 | convolution fusion | flops 1907855360 | bytes 14475276 | tf_op jit(solution)/shard_map/ild,df->ilf/dot_general | solution.py:388
  254.4 3.5 fusion.32
  257.9 0.0 copy-done.14
  257.9 7.0 %fusion.1 = bf16[2432,1216]{0,1:T(8,128)(2,1)} fusion(bf16[1,320,2432]{2,1,0:T(8,128)(2,1)S(1)} %get-tuple-element.18, bf16[1,320,2432]{2,1,0:T(8,128)(2,1)S(1)} %get-tuple-element.17, bf16[1,320,1216]{2,1,0:T(8,128)(2,1)S(1)} %copy-done.15, bf16[1,320,1216]{2,1,0:T(8,128)(2,1)S(1)} %copy-done.14), kind=kOutput, calls=%fused_computation.3 | convolution fusion | flops 3800612864 | bytes 10584064 | tf_op jit(solution)/shard_map/ild,ilf->df/dot_general | solution.py:402
  264.9 9.5 %copy.13 = bf16[2432,1216]{1,0:T(8,128)(2,1)} copy(bf16[2432,1216]{0,1:T(8,128)(2,1)} %fusion.1) | data formatting | bytes 11829248 | tf_op jit(solution)/shard_map/convert_element_type | solution.py:407
  274.5 8.4 %fusion = bf16[2432,1216]{0,1:T(8,128)(2,1)} fusion(bf16[1,320,2432]{2,1,0:T(8,128)(2,1)S(1)} %copy-done.13, bf16[1,320,2432]{2,1,0:T(8,128)(2,1)S(1)} %copy-done.11, bf16[1,320,1216]{2,1,0:T(8,128)(2,1)} %fusion.39, bf16[1,320,1216]{2,1,0:T(8,128)(2,1)} %fusion.38), kind=kOutput, calls=%fused_computation.2 | convolution fusion | flops 3800612864 | bytes 10584064 | tf_op jit(solution)/shard_map/ild,ilf->df/dot_general | solution.py:399
  282.9 9.4 %copy.12 = bf16[2432,1216]{1,0:T(8,128)(2,1)} copy(bf16[2432,1216]{0,1:T(8,128)(2,1)} %fusion) | data formatting | bytes 11829248 | tf_op jit(solution)/shard_map/convert_element_type | solution.py:407
  292.3 92.3 %update_weights.1 = (bf16[608,1216]{1,0:T(8,128)(2,1)}, bf16[608,1216]{1,0:T(8,128)(2,1)}) custom-call(bf16[4,608,1216]{2,1,0:T(8,128)(2,1)} %bitcast.154, bf16[4,608,1216]{2,1,0:T(8,128)(2,1)} %bitcast.153, bf16[608,1216]{1,0:T(8,128)(2,1)} %w_in.3, bf16[608,1216]{1,0:T(8,128)(2,1)} %w_down.3), custom_call_target="tpu_custom_call" | custom-call | tf_op jit(solution)/shard_map/update_weights/pallas_call | solution.py:291
  384.5 0.0 copy-start.1
  384.6 2.8 copy.29
  387.3 0.0 copy-done.9
  387.3 1.1 copy.30
  388.5 0.0 copy-done.1
  (27 shorter events, 0.1 us)
Async XLA Ops:
  0.6 6.7 %copy-start = (f32[10,2,2432]{2,1,0:T(2,128)S(1)}, f32[10,2,2432]{2,1,0:T(2,128)}, u32[]{:S(2)}) copy-start(f32[10,2,2432]{2,1,0:T(2,128)} %param.15) | copy-start | bytes 583684
  5.0 3.0 copy-start.2
  8.4 103.9 %copy-start.10 = (bf16[1,320,2432]{2,1,0:T(8,128)(2,1)}, bf16[1,320,2432]{2,1,0:T(8,128)(2,1)S(1)}, u32[]{:S(2)}) copy-start(bf16[1,320,2432]{2,1,0:T(8,128)(2,1)S(1)} %add_convert_fusion.1) | copy-start | bytes 4669444
  107.1 5.2 %copy-start.16 = (bf16[4,608,1216]{2,1,0:T(8,128)(2,1)S(1)}, bf16[4,608,1216]{2,1,0:T(8,128)(2,1)}, u32[]{:S(2)}) copy-start(bf16[4,608,1216]{2,1,0:T(8,128)(2,1)} %get-tuple-element.8) | copy-start | bytes 17743876
  169.0 2.4 copy-start.5
  169.1 12.8 %slice-start.2 = ((s8[6225920]{0:T(1024)(128)(4,1)}), s8[4194304]{0:T(1024)(128)(4,1)S(1)}, s32[]{:S(2)}) async-start(s8[6225920]{0:T(1024)(128)(4,1)} %bitcast.166), calls=%async_computation.2 | async-start | bytes 8388608
  171.4 10.5 %slice-start.3 = ((s8[6225920]{0:T(1024)(128)(4,1)}), s8[2031616]{0:T(1024)(128)(4,1)S(1)}, s32[]{:S(2)}) async-start(s8[6225920]{0:T(1024)(128)(4,1)} %bitcast.166), calls=%async_computation.3 | async-start | bytes 4063232
  180.2 1.7 copy-start.3
  180.2 6.5 %slice-start = ((s8[6225920]{0:T(1024)(128)(4,1)}), s8[4194304]{0:T(1024)(128)(4,1)S(1)}, s32[]{:S(2)}) async-start(s8[6225920]{0:T(1024)(128)(4,1)} %bitcast.162), calls=%async_computation | async-start | bytes 8388608
  181.9 2.4 copy-start.12
  181.9 4.9 %slice-start.1 = ((s8[6225920]{0:T(1024)(128)(4,1)}), s8[2031616]{0:T(1024)(128)(4,1)S(1)}, s32[]{:S(2)}) async-start(s8[6225920]{0:T(1024)(128)(4,1)} %bitcast.162), calls=%async_computation.1 | async-start | bytes 4063232
  184.2 2.5 copy-start.8
  190.3 56.1 %copy-start.7 = (bf16[1,2,320,2432]{3,2,1,0:T(8,128)(2,1)S(1)}, bf16[1,2,320,2432]{3,2,1,0:T(8,128)(2,1)}, u32[]{:S(2)}) copy-start(bf16[1,2,320,2432]{3,2,1,0:T(8,128)(2,1)} %param.11) | copy-start | bytes 9338884
  244.6 2.4 copy-start.6
  247.0 7.4 %copy-start.4 = (f32[1,320,2432]{2,1,0:T(8,128)S(1)}, f32[1,320,2432]{2,1,0:T(8,128)}, u32[]{:S(2)}) copy-start(f32[1,320,2432]{2,1,0:T(8,128)} %copy-done.3) | copy-start | bytes 9338884
  254.4 3.5 copy-start.14
  254.4 3.5 copy-start.15
  264.9 9.5 %copy-start.11 = (bf16[1,320,2432]{2,1,0:T(8,128)(2,1)S(1)}, bf16[1,320,2432]{2,1,0:T(8,128)(2,1)}, u32[]{:S(2)}) copy-start(bf16[1,320,2432]{2,1,0:T(8,128)(2,1)} %copy-done.10) | copy-start | bytes 4669444
  264.9 9.5 %copy-start.13 = (bf16[1,320,2432]{2,1,0:T(8,128)(2,1)S(1)}, bf16[1,320,2432]{2,1,0:T(8,128)(2,1)}, u32[]{:S(2)}) copy-start(bf16[1,320,2432]{2,1,0:T(8,128)(2,1)} %copy-done.12) | copy-start | bytes 4669444
  384.5 2.8 copy-start.9
  384.5 3.9 %copy-start.1 = (f32[10,2,2432]{2,1,0:T(2,128)S(1)}, f32[10,2,2432]{2,1,0:T(2,128)}, u32[]{:S(2)}) copy-start(f32[10,2,2432]{2,1,0:T(2,128)} %param.15) | copy-start | bytes 583684

commit v2 on v1

--- a/solution.py
+++ b/solution.py
@@ -46,70 +46,6 @@
     parts = 2 if rows % 32 == 0 else 1
     size = rows // parts
     return [pl.ds(c * size, size) for c in range(parts)]
-
-
-def gather_kernel(nd, w_in, w_down, out_in, out_down, xs, xr, fs, fr, os, orr, ls):
-    g, d = lax.axis_index("group"), lax.axis_index("dp")
-    other = 1 - g
-    targets = [lax.rem(d + o, nd) for o in range(nd)]
-    sources = [lax.rem(d - o + nd, nd) for o in range(nd)]
-    greet([{"group": other}] + [{"dp": targets[o]} for o in range(1, nd)])
-    chunks = row_chunks(w_in.shape[0])
-    mine = g * nd + d
-    pairs = ((w_in, out_in), (w_down, out_down))
-    pending = []
-    for a, (src, dst) in enumerate(pairs):
-        for c, rows in enumerate(chunks):
-            for o in range(1, nd):
-                copy = remote(src.at[rows], dst.at[mine, rows], xs.at[a, c, o], xr.at[a, c, o], dp=targets[o])
-                copy.start()
-                pending.append(copy)
-    local = []
-    for a, (src, dst) in enumerate(pairs):
-        copy = remote(src, dst.at[mine], os.at[a], orr.at[a], group=other)
-        copy.start()
-        pending.append(copy)
-        keep = pltpu.make_async_copy(src, dst.at[mine], ls.at[a])
-        keep.start()
-        local.append(keep)
-    for a, (src, dst) in enumerate(pairs):
-        for c, rows in enumerate(chunks):
-            for o in range(1, nd):
-                block = g * nd + sources[o]
-                remote(src.at[rows], dst.at[block, rows], xs.at[a, c, o], xr.at[a, c, o], dp=targets[o]).wait_recv()
-                copy = remote(dst.at[block, rows], dst.at[block, rows], fs.at[a, c, o], fr.at[a, c, o], group=other)
-                copy.start()
-                pending.append(copy)
-    for a, (src, dst) in enumerate(pairs):
-        remote(src, dst.at[other * nd + d], os.at[a], orr.at[a], group=other).wait_recv()
-        for c, rows in enumerate(chunks):
-            for o in range(1, nd):
-                block = other * nd + sources[o]
-                remote(dst.at[block, rows], dst.at[block, rows], fs.at[a, c, o], fr.at[a, c, o], group=other).wait_recv()
-    for copy in pending:
-        copy.wait_send()
-    for copy in local:
-        copy.wait()
-
-
-def gather_weights(w_in, w_down, ng, nd):
-    rows, units = w_in.shape
-    nc = len(row_chunks(rows))
-    dma = pltpu.SemaphoreType.DMA
-    shape = jax.ShapeDtypeStruct((ng * nd, rows, units), w_in.dtype)
-    full_in, full_down = pl.pallas_call(
-        functools.partial(gather_kernel, nd),
-        out_shape=(shape, shape),
-        in_specs=[pl.BlockSpec(memory_space=pl.ANY)] * 2,
-        out_specs=(pl.BlockSpec(memory_space=pl.ANY),) * 2,
-        scratch_shapes=[
-            dma((2, nc, nd)), dma((2, nc, nd)), dma((2, nc, nd)), dma((2, nc, nd)),
-            dma((2,)), dma((2,)), dma((2,)),
-        ],
-        compiler_params=params(1),
-        name="gather_weights",
-    )(w_in, w_down)
-    return full_in.reshape(ng * nd * rows, units), full_down.reshape(ng * nd * rows, units)
 
 
 def sum_kernel(no, src, out, ybuf, zsum, zbuf, ys, yr, zs, zr, gzs, gzr, gys, gyr):
@@ -175,8 +111,8 @@
 
 
 def update_kernel(
-    nd, n, count, g_in, g_down, w_in, w_down, new_in, new_down,
-    own, sib, far, total, sq_mp, sq_gd, cs, cr, xs, xr, ls, ms, mr, ps, pr,
+    nd, n, count, scales, lhs_down, rhs_down, lhs_in, rhs_in, w_down, w_in, new_down, new_in,
+    out_buf, sib, far, total, sq_mp, sq_gd, cs, cr, xs, xr, ms, mr, ps, pr,
 ):
     g, d, m = lax.axis_index("group"), lax.axis_index("dp"), lax.axis_index("mp")
     other = 1 - g
@@ -191,60 +127,65 @@
     rows = w_in.shape[0]
     chunks = row_chunks(rows)
     order = list(range(1, nd)) + [0]
-    grads = (g_in, g_down)
+    sides = ((lhs_down, rhs_down), (lhs_in, rhs_in))
     pending = []
-    loads = {}
+    far_sends = {}
+    step = 16 if chunks[0].size % 16 == 0 else chunks[0].size
+
+    def tiles(part, body, init):
+        return lax.fori_loop(
+            0, part.size // step,
+            lambda i, v: body(pl.ds(pl.multiple_of(part.start + i * step, step), step), v), init,
+        )
+
+    def block(a, index, part):
+        lhs, rhs = sides[a]
+        return jnp.dot(lhs[index, part], rhs[...], preferred_element_type=F32) * scales[a]
+
     for o in order:
         for a in range(2):
+            copies = []
             for c, part in enumerate(chunks):
+                out_buf[a, o, part] = block(a, other * nd + targets[o], part).astype(BF16)
                 copy = remote(
-                    grads[a].at[other * nd + targets[o], part], sib.at[a, o, part],
-                    cs.at[a, o, c], cr.at[a, o, c], group=other,
+                    out_buf.at[a, o, part], sib.at[a, o, part], cs.at[a, o, c], cr.at[a, o, c], group=other
                 )
                 copy.start()
-                pending.append(copy)
-                load = pltpu.make_async_copy(
-                    grads[a].at[g * nd + targets[o], part], own.at[a, o, part], ls.at[a, o, c]
-                )
-                load.start()
-                loads[a, o, c] = (load, copy)
-    step = 16
-    def tiles(part, body, init):
-        return lax.fori_loop(0, part.size // step, lambda i, v: body(pl.ds(pl.multiple_of(part.start + i * step, step), step), v), init)
-    for o in order[:-1]:
-        for a in range(2):
+                copies.append(copy)
             for c, part in enumerate(chunks):
-                load, copy = loads[a, o, c]
-                load.wait()
-                copy.wait_recv()
+                total[a, part] = block(a, g * nd + targets[o], part)
+                copies[c].wait_recv()
+
                 def add(at, _):
-                    sib[a, o, at] = (sib[a, o, at].astype(F32) + own[a, o, at].astype(F32)).astype(BF16)
+                    value = total[a, at] + sib[a, o, at].astype(F32)
+                    if o:
+                        sib[a, o, at] = value.astype(BF16)
+                    else:
+                        total[a, at] = value
                     return 0
+
                 tiles(part, add, 0)
-                send = remote(sib.at[a, o, part], far.at[a, o - 1, part], xs.at[a, o, c], xr.at[a, o, c], dp=targets[o])
-                send.start()
-                pending.append(send)
-                loads[a, o, c] = send
+                if o:
+                    send = remote(
+                        sib.at[a, o, part], far.at[a, o - 1, part], xs.at[a, o, c], xr.at[a, o, c], dp=targets[o]
+                    )
+                    send.start()
+                    pending.append(send)
+                    far_sends[a, o, c] = send
+            pending += copies
     square = jnp.zeros((step, w_in.shape[1]), F32)
     for a in range(2):
         for c, part in enumerate(chunks):
-            load, copy = loads[a, 0, c]
-            load.wait()
-            copy.wait_recv()
-            def near(at, _):
-                total[a, at] = sib[a, 0, at].astype(F32) + own[a, 0, at].astype(F32)
-                return 0
-            tiles(part, near, 0)
-    for a in range(2):
-        for c, part in enumerate(chunks):
             for o in order[:-1]:
-                loads[a, o, c].wait_recv()
+                far_sends[a, o, c].wait_recv()
+
             def finish(at, sq):
                 value = total[a, at]
                 for o in order[:-1]:
                     value = value + far[a, o - 1, at].astype(F32)
                 total[a, at] = value
                 return sq + value * value
+
             square = tiles(part, finish, square)
     sq_mp[0] = jnp.full((8, 128), jnp.sum(square), F32)
     sends = []
@@ -271,27 +212,29 @@
     for p in range(1, len(gd_peers)):
         value = value + sq_gd[p]
     inverse = lax.rsqrt(value[0:1, 0:1] / count + 1e-06)
-    for a, (w, new) in enumerate(((w_in, new_in), (w_down, new_down))):
+    for a, (w, new) in enumerate(((w_down, new_down), (w_in, new_in))):
+
         def update(at, _):
             new[at] = (w[at].astype(F32) - total[a, at] * inverse).astype(BF16)
             return 0
+
         tiles(pl.ds(0, rows), update, 0)
     for copy in pending:
         copy.wait_send()
 
 
-def update_weights(grad_in, grad_down, w_in, w_down, ng, nd, n):
+def update_weights(inputs, pre, vgrad, hidden, w_in, w_down, ng, nd, n, scales):
     rows, units = w_in.shape
     nc = len(row_chunks(rows))
     count = 2.0 * rows * ng * nd * units * n
     dma = pltpu.SemaphoreType.DMA
     vmem = pl.BlockSpec(memory_space=pltpu.VMEM)
-    hbm = pl.BlockSpec(memory_space=pl.ANY)
     shape = jax.ShapeDtypeStruct((rows, units), w_in.dtype)
-    return pl.pallas_call(
-        functools.partial(update_kernel, nd, n, count),
+    turned = lambda x: x.reshape(-1, x.shape[-1]).T.reshape(ng * nd, rows, -1)
+    new_down, new_in = pl.pallas_call(
+        functools.partial(update_kernel, nd, n, count, scales),
         out_shape=(shape, shape),
-        in_specs=[hbm, hbm, vmem, vmem],
+        in_specs=[vmem] * 6,
         out_specs=(vmem, vmem),
         scratch_shapes=[
             pltpu.VMEM((2, nd, rows, units), BF16),
@@ -300,20 +243,27 @@
             pltpu.VMEM((2, rows, units), F32),
             pltpu.VMEM((n, 8, 128), F32),
             pltpu.VMEM((ng * nd, 8, 128), F32),
-            dma((2, nd, nc)), dma((2, nd, nc)), dma((2, nd, nc)), dma((2, nd, nc)), dma((2, nd, nc)),
+            dma((2, nd, nc)), dma((2, nd, nc)), dma((2, nd, nc)), dma((2, nd, nc)),
             dma((n,)), dma((n,)), dma((ng * nd,)), dma((ng * nd,)),
         ],
         compiler_params=params(4),
         name="update_weights",
-    )(grad_in.reshape(ng * nd, rows, units), grad_down.reshape(ng * nd, rows, units), w_in, w_down)
-
-
-def update_by_ops(grad_in, grad_down, w_in, w_down, ng, nd, n):
+    )(
+        turned(vgrad), hidden.reshape(-1, units), turned(inputs), pre.reshape(-1, units), w_down, w_in
+    )
+    return new_in, new_down
+
+
+def update_by_ops(inputs, pre, vgrad, hidden, w_in, w_down, ng, nd, n, scales):
     rows, units = w_in.shape
     count = 2.0 * rows * ng * nd * units * n
+    grads = (
+        jnp.einsum("ild,ilf->df", inputs, pre, preferred_element_type=F32) * scales[1],
+        jnp.einsum("ild,ilf->df", vgrad, hidden, preferred_element_type=F32) * scales[0],
+    )
     mine = [
-        lax.psum_scatter(grad, ("group", "dp"), scatter_dimension=0, tiled=True).astype(F32)
-        for grad in (grad_in, grad_down)
+        lax.psum_scatter(grad.astype(BF16), ("group", "dp"), scatter_dimension=0, tiled=True).astype(F32)
+        for grad in grads
     ]
     total = lax.psum(sum(jnp.sum(grad * grad) for grad in mine), ("group", "dp", "mp"))
     rms = jnp.sqrt(total / count + 1e-06)
@@ -340,7 +290,10 @@
     hidden_width = shard_units * n
     step_len = 1.0 / SCHED
     vel_coef = 1.0 + 0.5 * NOISE_SLOPE * NOISE_SLOPE
-    w_in_full, w_down_full = gather_weights(w_in, w_down, ng, nd)
+    w_in_full, w_down_full = (
+        lax.all_gather(w_in, ("group", "dp"), axis=0, tiled=True),
+        lax.all_gather(w_down, ("group", "dp"), axis=0, tiled=True),
+    )
     latent_now = latents
     input_list = []
     hidden_list = []
@@ -396,15 +349,12 @@
     pre_all = jnp.concatenate(pre_list, axis=1)
     vgrad_all = jnp.concatenate(vgrad_list, axis=1)
     hidden_all = jnp.concatenate(hidden_list, axis=1)
-    grad_in = jnp.einsum(
-        "ild,ilf->df", inputs_all, pre_all, preferred_element_type=jnp.float32
-    ) / math.sqrt(model_width)
-    grad_down = jnp.einsum(
-        "ild,ilf->df", vgrad_all, hidden_all, preferred_element_type=jnp.float32
-    ) / math.sqrt(hidden_width)
-    held = 6 * nd * w_in.size * 2 + 4 * w_in.size * 4
-    update = update_weights if held < VMEM_LIMIT * 3 // 4 else update_by_ops
-    new_in, new_down = update(grad_in.astype(BF16), grad_down.astype(BF16), w_in, w_down, ng, nd, n)
+    held = (6 * nd + 6) * w_in.size * 2 + 2 * (inputs_all.size + pre_all.size) * 2
+    update = update_weights if held < VMEM_LIMIT * 7 // 8 else update_by_ops
+    scales = (1.0 / math.sqrt(hidden_width), 1.0 / math.sqrt(model_width))
+    new_in, new_down = update(
+        inputs_all, pre_all, vgrad_all, hidden_all, w_in, w_down, ng, nd, n, scales
+    )
     return (latent_now, new_in, new_down)
 
 

time: 389 us -> 381 us (0.979)
  Pallas kernels: 298 us -> 204 us
  waiting for transfers between devices: 0 us -> 84.3 us
  matrix products: 45.8 us -> 31.4 us
  between operations: 3.93 us -> 17.3 us
  other arithmetic: 13.8 us -> 24 us
  local copies, waits for them, and re-layouts: 26.5 us -> 19.1 us
    pallas_call x2 -> x1, Pallas kernels: 191 us -> 95.7 us  [update_weights(): pl.pallas_call(functools.partial(update_kernel, nd, n, count, scales), ou...]
    all_gather x0 -> x2, waiting for transfers between devices: none -> 82.9 us  [the longest x1 43.6 us: on_device(): lax.all_gather(w_in, ('group', 'dp'), axis=0, tiled=True)]
    convert_element_type x2 -> x0, local copies, waits for them, and re-layouts: 18.9 us -> none  [the longest x1 9.52 us: on_device(): grad_down.astype(BF16)]
    dot_general x2 -> x0, matrix products: 15.5 us -> none  [the longest x1 8.41 us: on_device(): jnp.einsum('ild,ilf->df', inputs_all, pre_all, preferred_element_type=jnp...]
    transpose x0 -> x2, local copies, waits for them, and re-layouts: none -> 9.22 us  [update_weights(): turned = lambda x: x.reshape(-1, x.shape[-1]).T.reshape(ng * nd, rows, -1)]
    convert_element_type x1 -> x2, other arithmetic: 3.5 us -> 8.31 us  [on_device(): vel_grad = (pg_coef * vel_coef * math.sqrt(step_len) * eps_draw / noise_l...]
    unnamed x44 -> x48, local copies, waits for them, and re-layouts: 6.32 us -> 9.34 us
  transfers between devices with their start and end apart: 0 -> 2, of which waited for: 0 -> 2; matrix products, arithmetic and copies ran while one was open for 0% -> 3% of each run, Pallas kernels for 0% -> 0%
where the time goes in v2:
time: 381 us; the launch traced here: 380 us
  Pallas kernels  204 us (54%)
  waiting for transfers between devices  84.3 us (22%)
  matrix products  31.4 us (8%)
  other arithmetic  24 us (6%)
  local copies, waits for them, and re-layouts  19.1 us (5%)
  between operations  17.3 us (5%)
    pallas_call x2, Pallas kernels, sum_over_mp(): pl.pallas_call(functools.partial(sum_kernel, no), out_shape=jax.ShapeDtyp...  108 us
    pallas_call x1, Pallas kernels, update_weights(): pl.pallas_call(functools.partial(update_kernel, nd, n, count, scales), ou...  95.7 us
    all_gather x1, waiting for transfers between devices, on_device(): lax.all_gather(w_in, ('group', 'dp'), axis=0, tiled=True)  43.6 us
    all_gather x1, waiting for transfers between devices, on_device(): lax.all_gather(w_down, ('group', 'dp'), axis=0, tiled=True)  39.3 us
    dot_general x2, matrix products, on_device(): jnp.einsum('ild,df->ilf', vel_grad, w_down_full, preferred_element_type=j...  12.5 us
    dot_general x2, matrix products, on_device(): jnp.einsum('ilf,df->ild', hidden, w_down_full, preferred_element_type=jnp...  10.6 us
    unnamed x48, local copies, waits for them, and re-layouts  9.34 us
    transpose x2, local copies, waits for them, and re-layouts, update_weights(): turned = lambda x: x.reshape(-1, x.shape[-1]).T.reshape(ng * nd, rows, -1)  9.22 us
  transfers between devices with their start and end apart: 2, of which 2 were waited for; matrix products, arithmetic and copies ran while one was open for 3% of the time, Pallas kernels for 0%

profile of v2, /device:TPU:0, one launch (start us, length us, event | category | flops | bytes accessed | tf_op | source)
XLA Modules:
  0.0 380.4 jit_solution(5022626342398210141)
XLA Ops:
  7.2 0.0 copy-start
  7.2 0.0 all-gather.3.cloned.1.call-start
  7.2 0.7 all-gather.3.cloned.1.call-update
  7.9 0.0 all-gather.5.cloned.1.call-start
  8.0 0.7 all-gather.5.cloned.1.call-update
  9.3 0.6 fusion.67
  12.3 0.2 fusion.48
  12.5 0.1 fusion.55
  12.6 0.2 fusion.46
  12.8 0.1 fusion.52
  12.9 0.3 multiply_reduce_fusion.1
  13.2 1.6 add_convert_fusion.1
  14.8 43.6 %all-gather.3.cloned.1.call-done = bf16[2432,1216]{1,0:T(8,128)(2,1)} async-done(((bf16[608,1216]{1,0:T(8,128)(2,1)}), bf16[2432,1216]{1,0:T(8,128)(2,1)}) %all-gather.3.cloned.1.call-update) | async-done | bytes 5914640 | tf_op jit(solution)/shard_map/all_gather | solution.py:294
  58.3 5.5 %fusion.44 = f32[320,1216]{1,0:T(8,128)S(1)} fusion(bf16[2432,1216]{1,0:T(8,128)(2,1)} %all-gather.3.cloned.1.call-done, bf16[1,320,2432]{2,1,0:T(8,128)(2,1)} %add_convert_fusion.1), kind=kOutput, calls=%fused_computation.70 | convolution fusion | flops 1892679680 | bytes 9027584 | tf_op jit(solution)/shard_map/ild,df->ilf/dot_general | solution.py:315
  63.9 1.3 copy-done.13
  65.1 1.5 fusion.64
  66.6 39.3 %all-gather.5.cloned.1.call-done = bf16[2432,1216]{1,0:T(8,128)(2,1)} async-done(((bf16[608,1216]{1,0:T(8,128)(2,1)}), bf16[2432,1216]{1,0:T(8,128)(2,1)}) %all-gather.5.cloned.1.call-update) | async-done | bytes 5914640 | tf_op jit(solution)/shard_map/all_gather | solution.py:295
  105.9 6.8 %fusion = bf16[320,2432]{1,0:T(8,128)(2,1)} fusion(bf16[2432,1216]{1,0:T(8,128)(2,1)} %all-gather.5.cloned.1.call-done, f32[320,1216]{1,0:T(8,128)} %copy-done.13), kind=kOutput, calls=%fused_computation.2 | convolution fusion | flops 1898127360 | bytes 9027584 | tf_op jit(solution)/shard_map/ilf,df->ild/dot_general | solution.py:320
  112.8 53.5 %sum_over_mp.2 = bf16[8,40,2432]{2,1,0:T(8,128)(2,1)} custom-call(bf16[8,40,2432]{2,1,0:T(8,128)(2,1)} %bitcast.187), custom_call_target="tpu_custom_call" | custom-call | tf_op jit(solution)/shard_map/sum_over_mp/pallas_call | solution.py:101
  166.2 0.0 copy-start.5
  166.3 1.8 convert_element_type.234
  168.0 0.6 copy-done.5
  168.6 1.0 multiply_reduce_fusion
  169.7 0.4 add_convert_fusion
  170.1 1.2 copy-done.3
  171.3 1.1 copy-done.10
  172.4 1.9 maximum_bitcast_fusion.1
  174.3 2.3 fusion.42
  176.6 1.5 fusion.65
  178.1 3.8 fusion.1
  181.9 55.0 %sum_over_mp.3 = bf16[8,40,2432]{2,1,0:T(8,128)(2,1)} custom-call(bf16[8,40,2432]{2,1,0:T(8,128)(2,1)} %bitcast.188), custom_call_target="tpu_custom_call" | custom-call | tf_op jit(solution)/shard_map/sum_over_mp/pallas_call | solution.py:101
  236.9 0.0 copy-start.6
  237.0 1.8 convert_element_type.235
  238.7 0.6 copy-done.6
  239.3 0.5 copy-done.7
  239.7 4.8 %fusion.28 = (bf16[320,2432]{1,0:T(8,128)(2,1)}, bf16[320,2432]{1,0:T(8,128)(2,1)}) fusion(f32[]{:T(128)} %bitcast.23, f32[]{:T(128)} %bitcast.20, f32[]{:T(128)} %bitcast.19, bf16[1,2,320,2432]{3,2,1,0:T(8,128)(2,1)} %param.11, bf16[1,2,320,2432]{3,2,1,0:T(8,128)(2,1)S(1)} %copy-done.6, bf16[8,40,2432]{2,1,0:T(8,128)(2,1)S(1)} %copy-done.7, f32[]{:T(128)} %bitcast.29, ...), kind=kLoop, calls=%fused_computation.46 | loop fusion | flops 15564800 | bytes 12451864 | tf_op jit(solution)/shard_map/convert_element_type | solution.py:340
  244.6 0.2 copy-done.9
  244.8 3.5 fusion.29
  248.3 1.8 maximum_bitcast_fusion
  250.1 5.7 %copy.12 = bf16[2432,640]{1,0:T(8,128)(2,1)} copy(bf16[2432,640]{0,1:T(8,128)(2,1)} %maximum_bitcast_fusion) | data formatting | bytes 6225920 | tf_op jit(solution)/shard_map/transpose | solution.py:233
  255.8 3.5 copy.13
  259.3 6.7 %fusion.35 = bf16[1,320,1216]{2,1,0:T(8,128)(2,1)S(1)} fusion(bf16[320,2432]{1,0:T(8,128)(2,1)} %get-tuple-element.14, bf16[2432,1216]{1,0:T(8,128)(2,1)} %all-gather.5.cloned.1.call-done, f32[320,1216]{1,0:T(8,128)} %copy-done.15), kind=kOutput, calls=%fused_computation.55 | convolution fusion | flops 1900851200 | bytes 9805824 | tf_op jit(solution)/shard_map/ild,df->ilf/dot_general | solution.py:341
  266.1 5.8 %fusion.34 = bf16[1,320,1216]{2,1,0:T(8,128)(2,1)S(1)} fusion(bf16[320,2432]{1,0:T(8,128)(2,1)S(1)} %copy-done.17, bf16[2432,1216]{1,0:T(8,128)(2,1)} %all-gather.5.cloned.1.call-done, f32[320,1216]{1,0:T(8,128)S(1)} %copy-done.14), kind=kOutput, calls=%fused_computation.54 | convolution fusion | flops 1900851200 | bytes 9805824 | tf_op jit(solution)/shard_map/ild,df->ilf/dot_general | solution.py:341
  271.9 2.1 maximum_bitcast_fusion.2
  273.9 95.7 %update_weights.1 = (bf16[608,1216]{1,0:T(8,128)(2,1)}, bf16[608,1216]{1,0:T(8,128)(2,1)}) custom-call(bf16[4,608,640]{2,1,0:T(8,128)(2,1)} %bitcast.184, bf16[640,1216]{1,0:T(8,128)(2,1)} %get-tuple-element.20.rhs_down, bf16[4,608,640]{2,1,0:T(8,128)(2,1)} %bitcast.185, bf16[640,1216]{1,0:T(8,128)(2,1)} %get-tuple-element.21.rhs_in, ...), custom_call_target="tpu_custom_call" | custom-call | tf_op jit(solution)/shard_map/update_weights/pallas_call | solution.py:234
  369.7 0.0 copy-start.1
  369.7 2.8 copy.29
  372.4 1.1 copy.30
  (39 shorter events, 0.1 us)
Async XLA Ops:
  7.2 5.1 %copy-start = (f32[10,2,2432]{2,1,0:T(2,128)S(1)}, f32[10,2,2432]{2,1,0:T(2,128)}, u32[]{:S(2)}) copy-start(f32[10,2,2432]{2,1,0:T(2,128)} %param.15) | copy-start | bytes 583684
  7.2 2.2 copy-start.18
  7.2 5.7 %copy-start.2 = (f32[1,320,2432]{2,1,0:T(8,128)S(1)}, f32[1,320,2432]{2,1,0:T(8,128)}, u32[]{:S(2)}) copy-start(f32[1,320,2432]{2,1,0:T(8,128)} %param.9) | copy-start | bytes 9338884
  7.2 51.1 %all-gather.3.cloned.1.call-start = ((), (), s32[]{:S(2)}) async-start(), calls=%async_computation | async-start | bytes 7782400 | tf_op jit(solution)/shard_map/all_gather | solution.py:294
  7.9 98.0 %all-gather.5.cloned.1.call-start = ((), (), s32[]{:S(2)}) async-start(), calls=%async_computation.1 | async-start | bytes 7782400 | tf_op jit(solution)/shard_map/all_gather | solution.py:295
  63.9 1.3 copy-start.13
  166.2 2.4 copy-start.5
  168.6 5.7 %slice-start.2 = ((s8[6225920]{0:T(1024)(128)(4,1)}), s8[4194304]{0:T(1024)(128)(4,1)S(1)}, s32[]{:S(2)}) async-start(s8[6225920]{0:T(1024)(128)(4,1)} %bitcast.191), calls=%async_computation.4 | async-start | bytes 8388608
  169.6 1.7 copy-start.3
  169.6 2.7 copy-start.10
  169.7 4.6 %slice-start.3 = ((s8[6225920]{0:T(1024)(128)(4,1)}), s8[2031616]{0:T(1024)(128)(4,1)S(1)}, s32[]{:S(2)}) async-start(s8[6225920]{0:T(1024)(128)(4,1)} %bitcast.191), calls=%async_computation.5 | async-start | bytes 4063232
  172.4 5.7 %slice-start = ((s8[6225920]{0:T(1024)(128)(4,1)}), s8[4194304]{0:T(1024)(128)(4,1)S(1)}, s32[]{:S(2)}) async-start(s8[6225920]{0:T(1024)(128)(4,1)} %bitcast.189), calls=%async_computation.2 | async-start | bytes 8388608
  174.3 3.8 %slice-start.1 = ((s8[6225920]{0:T(1024)(128)(4,1)}), s8[2031616]{0:T(1024)(128)(4,1)S(1)}, s32[]{:S(2)}) async-start(s8[6225920]{0:T(1024)(128)(4,1)} %bitcast.189), calls=%async_computation.3 | async-start | bytes 4063232
  176.6 5.3 %copy-start.15 = (f32[320,1216]{1,0:T(8,128)}, f32[320,1216]{1,0:T(8,128)S(1)}, u32[]{:S(2)}) copy-start(f32[320,1216]{1,0:T(8,128)S(1)} %fusion.42) | copy-start | bytes 4669444
  236.9 2.4 copy-start.6
  236.9 2.8 copy-start.7
  239.7 4.8 %copy-start.4 = (f32[1,320,2432]{2,1,0:T(8,128)S(1)}, f32[1,320,2432]{2,1,0:T(8,128)}, u32[]{:S(2)}) copy-start(f32[1,320,2432]{2,1,0:T(8,128)} %copy-done.3) | copy-start | bytes 9338884
  239.7 5.0 %copy-start.9 = (bf16[1,2,320,2432]{3,2,1,0:T(8,128)(2,1)S(1)}, bf16[1,2,320,2432]{3,2,1,0:T(8,128)(2,1)}, u32[]{:S(2)}) copy-start(bf16[1,2,320,2432]{3,2,1,0:T(8,128)(2,1)} %param.11) | copy-start | bytes 9338884
  250.1 5.7 %copy-start.8 = (bf16[2432,640]{0,1:T(8,128)(2,1)S(1)}, bf16[2432,640]{0,1:T(8,128)(2,1)}, u32[]{:S(2)}) copy-start(bf16[2432,640]{0,1:T(8,128)(2,1)} %maximum_bitcast_fusion.1) | copy-start | bytes 9338884
  259.3 6.7 %copy-start.14 = (f32[320,1216]{1,0:T(8,128)S(1)}, f32[320,1216]{1,0:T(8,128)}, u32[]{:S(2)}) copy-start(f32[320,1216]{1,0:T(8,128)} %copy-done.13) | copy-start | bytes 4669444
  259.3 6.7 %copy-start.17 = (bf16[320,2432]{1,0:T(8,128)(2,1)S(1)}, bf16[320,2432]{1,0:T(8,128)(2,1)}, u32[]{:S(2)}) copy-start(bf16[320,2432]{1,0:T(8,128)(2,1)} %get-tuple-element.13) | copy-start | bytes 4669444
  266.0 5.8 %copy-start.11 = (bf16[1,320,1216]{2,1,0:T(8,128)(2,1)S(1)}, bf16[1,320,1216]{2,1,0:T(8,128)(2,1)}, u32[]{:S(2)}) copy-start(bf16[1,320,1216]{2,1,0:T(8,128)(2,1)} %fusion.64) | copy-start | bytes 2334724
  266.0 5.8 %copy-start.12 = (bf16[1,320,1216]{2,1,0:T(8,128)(2,1)S(1)}, bf16[1,320,1216]{2,1,0:T(8,128)(2,1)}, u32[]{:S(2)}) copy-start(bf16[1,320,1216]{2,1,0:T(8,128)(2,1)} %fusion.65) | copy-start | bytes 2334724
  369.6 2.8 copy-start.16
  369.7 3.9 %copy-start.1 = (f32[10,2,2432]{2,1,0:T(2,128)S(1)}, f32[10,2,2432]{2,1,0:T(2,128)}, u32[]{:S(2)}) copy-start(f32[10,2,2432]{2,1,0:T(2,128)} %param.15) | copy-start | bytes 583684
Sparse Core Ops, SparseCore 0:
  9.6 48.6 all-gather.2
  59.9 45.9 all-gather.4

commit v3 on v2

--- a/solution.py
+++ b/solution.py
@@ -112,7 +112,7 @@
 
 def update_kernel(
     nd, n, count, scales, lhs_down, rhs_down, lhs_in, rhs_in, w_down, w_in, new_down, new_in,
-    out_buf, sib, far, total, sq_mp, sq_gd, cs, cr, xs, xr, ms, mr, ps, pr,
+    turned, out_buf, sib, far, total, sq_mp, sq_gd, cs, cr, xs, xr, ms, mr, ps, pr,
 ):
     g, d, m = lax.axis_index("group"), lax.axis_index("dp"), lax.axis_index("mp")
     other = 1 - g
@@ -139,12 +139,24 @@
         )
 
     def block(a, index, part):
-        lhs, rhs = sides[a]
-        return jnp.dot(lhs[index, part], rhs[...], preferred_element_type=F32) * scales[a]
+        at = pl.ds(pl.multiple_of(index * rows + part.start, 8), part.size)
+        return jnp.dot(turned[a, at], sides[a][1][...], preferred_element_type=F32) * scales[a]
+
+    def turn(a):
+        lhs = sides[a][0]
+
+        def body(t, _):
+            at = pl.ds(pl.multiple_of(t * 128, 128), 128)
+            turned[a, at] = lhs[:, at].T
+            return 0
+
+        lax.fori_loop(0, lhs.shape[1] // 128, body, 0)
 
     for o in order:
         for a in range(2):
             copies = []
+            if o == order[0]:
+                turn(a)
             for c, part in enumerate(chunks):
                 out_buf[a, o, part] = block(a, other * nd + targets[o], part).astype(BF16)
                 copy = remote(
@@ -230,13 +242,15 @@
     dma = pltpu.SemaphoreType.DMA
     vmem = pl.BlockSpec(memory_space=pltpu.VMEM)
     shape = jax.ShapeDtypeStruct((rows, units), w_in.dtype)
-    turned = lambda x: x.reshape(-1, x.shape[-1]).T.reshape(ng * nd, rows, -1)
+    flat = lambda x: x.reshape(-1, x.shape[-1])
+    tokens = flat(inputs).shape[0]
     new_down, new_in = pl.pallas_call(
         functools.partial(update_kernel, nd, n, count, scales),
         out_shape=(shape, shape),
         in_specs=[vmem] * 6,
         out_specs=(vmem, vmem),
         scratch_shapes=[
+            pltpu.VMEM((2, ng * nd * rows, tokens), BF16),
             pltpu.VMEM((2, nd, rows, units), BF16),
             pltpu.VMEM((2, nd, rows, units), BF16),
             pltpu.VMEM((2, nd - 1, rows, units), BF16),
@@ -249,7 +263,7 @@
         compiler_params=params(4),
         name="update_weights",
     )(
-        turned(vgrad), hidden.reshape(-1, units), turned(inputs), pre.reshape(-1, units), w_down, w_in
+        flat(vgrad), flat(hidden), flat(inputs), flat(pre), w_down, w_in
     )
     return new_in, new_down
 
@@ -349,7 +363,7 @@
     pre_all = jnp.concatenate(pre_list, axis=1)
     vgrad_all = jnp.concatenate(vgrad_list, axis=1)
     hidden_all = jnp.concatenate(hidden_list, axis=1)
-    held = (6 * nd + 6) * w_in.size * 2 + 2 * (inputs_all.size + pre_all.size) * 2
+    held = (6 * nd + 6) * w_in.size * 2 + 2 * (2 * inputs_all.size + pre_all.size) * 2
     update = update_weights if held < VMEM_LIMIT * 7 // 8 else update_by_ops
     scales = (1.0 / math.sqrt(hidden_width), 1.0 / math.sqrt(model_width))
     new_in, new_down = update(

time: 381 us -> 367 us (0.963)
  local copies, waits for them, and re-layouts: 19.1 us -> 9.04 us
  matrix products: 31.4 us -> 24.7 us
    transpose x2 -> x0, local copies, waits for them, and re-layouts: 9.22 us -> none  [update_weights(): turned = lambda x: x.reshape(-1, x.shape[-1]).T.reshape(ng * nd, rows, -1)]
    dot_general x2, matrix products: 12.5 us -> 5.77 us  [on_device(): jnp.einsum('ild,df->ilf', vel_grad, w_down_full, preferred_element_type=j...]
    reshape x1 -> x2, other arithmetic: 2.05 us -> 8.03 us  [update_weights(): flat = lambda x: x.reshape(-1, x.shape[-1])]
    unnamed x48 -> x50, local copies, waits for them, and re-layouts: 9.34 us -> 8.45 us
where the time goes in v3:
time: 367 us
  Pallas kernels  206 us (56%)
  waiting for transfers between devices  84.3 us (23%)
  other arithmetic  25.2 us (7%)
  matrix products  24.7 us (7%)
  between operations  17.3 us (5%)
  local copies, waits for them, and re-layouts  9.04 us (2%)
    pallas_call x2, Pallas kernels, sum_over_mp(): pl.pallas_call(functools.partial(sum_kernel, no), out_shape=jax.ShapeDtyp...  109 us
    pallas_call x1, Pallas kernels, update_weights(): pl.pallas_call(functools.partial(update_kernel, nd, n, count, scales), ou...  97.9 us
    all_gather x1, waiting for transfers between devices, on_device(): lax.all_gather(w_in, ('group', 'dp'), axis=0, tiled=True)  43.6 us
    all_gather x1, waiting for transfers between devices, on_device(): lax.all_gather(w_down, ('group', 'dp'), axis=0, tiled=True)  39.4 us
    dot_general x2, matrix products, on_device(): jnp.einsum('ilf,df->ild', hidden, w_down_full, preferred_element_type=jnp...  10.6 us
    unnamed x50, local copies, waits for them, and re-layouts  8.45 us
    reshape x2, other arithmetic, update_weights(): flat = lambda x: x.reshape(-1, x.shape[-1])  8.03 us
    dot_general x2, matrix products, on_device(): jnp.einsum('ild,df->ilf', inputs, w_in_full, preferred_element_type=jnp.f...  7.83 us
  transfers between devices with their start and end apart: 2, of which 2 were waited for; matrix products, arithmetic and copies ran while one was open for 3% of the time, Pallas kernels for 0%

profile of v3, /device:TPU:0, one launch (start us, length us, event | category | flops | bytes accessed | tf_op | source)
XLA Modules:
  0.0 367.1 jit_solution(11745359049766643111)
XLA Ops:
  7.2 0.0 copy-start
  7.2 0.0 all-gather.3.cloned.1.call-start
  7.2 0.7 all-gather.3.cloned.1.call-update
  7.9 0.0 all-gather.5.cloned.1.call-start
  8.0 0.7 all-gather.5.cloned.1.call-update
  9.3 0.6 fusion.67
  12.3 0.0 copy-done
  12.3 0.2 fusion.48
  12.5 0.1 fusion.55
  12.6 0.2 fusion.46
  12.8 0.1 fusion.52
  12.9 0.0 copy-done.2
  12.9 0.3 multiply_reduce_fusion.1
  13.2 1.6 add_convert_fusion.1
  14.8 43.6 %all-gather.3.cloned.1.call-done = bf16[2432,1216]{1,0:T(8,128)(2,1)} async-done(((bf16[608,1216]{1,0:T(8,128)(2,1)}), bf16[2432,1216]{1,0:T(8,128)(2,1)}) %all-gather.3.cloned.1.call-update) | async-done | bytes 5914640 | tf_op jit(solution)/shard_map/all_gather | solution.py:308
  58.3 5.5 %fusion.44 = f32[320,1216]{1,0:T(8,128)S(1)} fusion(bf16[2432,1216]{1,0:T(8,128)(2,1)} %all-gather.3.cloned.1.call-done, bf16[1,320,2432]{2,1,0:T(8,128)(2,1)} %add_convert_fusion.1), kind=kOutput, calls=%fused_computation.70 | convolution fusion | flops 1892679680 | bytes 9027584 | tf_op jit(solution)/shard_map/ild,df->ilf/dot_general | solution.py:329
  63.9 1.2 copy-done.12
  65.0 1.5 fusion.64
  66.5 39.4 %all-gather.5.cloned.1.call-done = bf16[2432,1216]{1,0:T(8,128)(2,1)} async-done(((bf16[608,1216]{1,0:T(8,128)(2,1)}), bf16[2432,1216]{1,0:T(8,128)(2,1)}) %all-gather.5.cloned.1.call-update) | async-done | bytes 5914640 | tf_op jit(solution)/shard_map/all_gather | solution.py:309
  105.9 6.8 %fusion = bf16[320,2432]{1,0:T(8,128)(2,1)} fusion(bf16[2432,1216]{1,0:T(8,128)(2,1)} %all-gather.5.cloned.1.call-done, f32[320,1216]{1,0:T(8,128)} %copy-done.12), kind=kOutput, calls=%fused_computation.2 | convolution fusion | flops 1898127360 | bytes 9027584 | tf_op jit(solution)/shard_map/ilf,df->ild/dot_general | solution.py:334
  112.8 53.5 %sum_over_mp.2 = bf16[8,40,2432]{2,1,0:T(8,128)(2,1)} custom-call(bf16[8,40,2432]{2,1,0:T(8,128)(2,1)} %bitcast.179), custom_call_target="tpu_custom_call" | custom-call | tf_op jit(solution)/shard_map/sum_over_mp/pallas_call | solution.py:101
  166.2 0.0 copy-start.5
  166.3 0.0 slice-start.4
  166.3 1.8 convert_element_type.234
  168.0 0.6 copy-done.5
  168.6 1.0 multiply_reduce_fusion
  169.7 0.0 slice-start
  169.7 0.4 add_convert_fusion
  170.1 1.2 copy-done.3
  171.3 2.3 fusion.42
  173.6 1.5 fusion.65
  175.1 3.8 %fusion.1 = bf16[320,2432]{1,0:T(8,128)(2,1)} fusion(bf16[2432,1216]{1,0:T(8,128)(2,1)S(1)} %bitcast.182, f32[320,1216]{1,0:T(8,128)S(1)} %fusion.42), kind=kOutput, calls=%fused_computation.3 | convolution fusion | flops 1898127360 | bytes 9027584 | tf_op jit(solution)/shard_map/ilf,df->ild/dot_general | solution.py:334
  178.9 55.1 %sum_over_mp.3 = bf16[8,40,2432]{2,1,0:T(8,128)(2,1)} custom-call(bf16[8,40,2432]{2,1,0:T(8,128)(2,1)} %bitcast.180), custom_call_target="tpu_custom_call" | custom-call | tf_op jit(solution)/shard_map/sum_over_mp/pallas_call | solution.py:101
  234.0 0.0 copy-start.6
  234.0 1.8 convert_element_type.235
  235.8 0.6 copy-done.6
  236.4 0.5 copy-done.7
  236.8 3.7 %fusion.28 = (bf16[320,2432]{1,0:T(8,128)(2,1)S(1)}, bf16[320,2432]{1,0:T(8,128)(2,1)S(1)}) fusion(f32[]{:T(128)} %bitcast.23, f32[]{:T(128)} %bitcast.20, f32[]{:T(128)} %bitcast.19, bf16[1,2,320,2432]{3,2,1,0:T(8,128)(2,1)} %param.11, bf16[1,2,320,2432]{3,2,1,0:T(8,128)(2,1)S(1)} %copy-done.6, bf16[8,40,2432]{2,1,0:T(8,128)(2,1)S(1)} %copy-done.7, ...), kind=kLoop, calls=%fused_computation.46 | loop fusion | flops 15564800 | bytes 12451864 | tf_op jit(solution)/shard_map/convert_element_type | solution.py:354
  240.5 0.5 copy-done.8
  241.1 3.5 fusion.29
  244.5 6.1 %maximum_bitcast_fusion = (bf16[640,2432]{1,0:T(8,128)(2,1)}, bf16[640,2432]{1,0:T(8,128)(2,1)}) fusion(bf16[1,320,2432]{2,1,0:T(8,128)(2,1)S(1)} %get-tuple-element.16, bf16[1,320,2432]{2,1,0:T(8,128)(2,1)S(1)} %get-tuple-element.15, bf16[1,320,2432]{2,1,0:T(8,128)(2,1)S(1)} %add_convert_fusion, bf16[1,320,2432]{2,1,0:T(8,128)(2,1)S(1)} %copy-done.9), kind=kLoop, calls=%fused_computation.34 | loop fusion | flops 12451840 | bytes 12451840 | tf_op jit(solution)/shard_map/reshape | solution.py:245
  250.7 2.9 fusion.35
  253.6 2.9 fusion.34
  256.5 2.0 maximum_bitcast_fusion.2
  258.4 97.9 %update_weights.1 = (bf16[608,1216]{1,0:T(8,128)(2,1)}, bf16[608,1216]{1,0:T(8,128)(2,1)}) custom-call(bf16[640,2432]{1,0:T(8,128)(2,1)} %get-tuple-element.20.lhs_down, bf16[640,1216]{1,0:T(8,128)(2,1)} %get-tuple-element.22.rhs_down, bf16[640,2432]{1,0:T(8,128)(2,1)} %get-tuple-element.21.lhs_in, bf16[640,1216]{1,0:T(8,128)(2,1)} %get-tuple-element.23.rhs_in, ...), custom_call_target="tpu_custom_call" | custom-call | tf_op jit(solution)/shard_map/update_weights/pallas_call | solution.py:247
  356.4 0.0 copy-start.1
  356.4 2.8 copy.27
  359.1 1.1 copy.28
  (39 shorter events, 0.1 us)
Async XLA Ops:
  7.2 5.1 %copy-start = (f32[10,2,2432]{2,1,0:T(2,128)S(1)}, f32[10,2,2432]{2,1,0:T(2,128)}, u32[]{:S(2)}) copy-start(f32[10,2,2432]{2,1,0:T(2,128)} %param.15) | copy-start | bytes 583684
  7.2 2.2 copy-start.17
  7.2 5.7 %copy-start.2 = (f32[1,320,2432]{2,1,0:T(8,128)S(1)}, f32[1,320,2432]{2,1,0:T(8,128)}, u32[]{:S(2)}) copy-start(f32[1,320,2432]{2,1,0:T(8,128)} %param.9) | copy-start | bytes 9338884
  7.2 51.1 %all-gather.3.cloned.1.call-start = ((), (), s32[]{:S(2)}) async-start(), calls=%async_computation | async-start | bytes 7782400 | tf_op jit(solution)/shard_map/all_gather | solution.py:308
  7.9 98.0 %all-gather.5.cloned.1.call-start = ((), (), s32[]{:S(2)}) async-start(), calls=%async_computation.1 | async-start | bytes 7782400 | tf_op jit(solution)/shard_map/all_gather | solution.py:309
  63.9 1.2 copy-start.12
  166.2 2.4 copy-start.5
  166.3 5.0 %slice-start.4 = ((s8[6225920]{0:T(1024)(128)(4,1)}), s8[4194304]{0:T(1024)(128)(4,1)S(1)}, s32[]{:S(2)}) async-start(s8[6225920]{0:T(1024)(128)(4,1)} %bitcast.185), calls=%async_computation.6 | async-start | bytes 8388608
  168.6 2.7 slice-start.5
  169.6 1.7 copy-start.3
  169.7 5.5 %slice-start = ((s8[6225920]{0:T(1024)(128)(4,1)}), s8[4194304]{0:T(1024)(128)(4,1)S(1)}, s32[]{:S(2)}) async-start(s8[6225920]{0:T(1024)(128)(4,1)} %bitcast.181), calls=%async_computation.2 | async-start | bytes 8388608
  171.3 3.8 %slice-start.1 = ((s8[6225920]{0:T(1024)(128)(4,1)}), s8[2031616]{0:T(1024)(128)(4,1)S(1)}, s32[]{:S(2)}) async-start(s8[6225920]{0:T(1024)(128)(4,1)} %bitcast.181), calls=%async_computation.3 | async-start | bytes 4063232
  173.6 5.3 %copy-start.14 = (f32[320,1216]{1,0:T(8,128)}, f32[320,1216]{1,0:T(8,128)S(1)}, u32[]{:S(2)}) copy-start(f32[320,1216]{1,0:T(8,128)S(1)} %fusion.42) | copy-start | bytes 4669444
  234.0 2.4 copy-start.6
  234.0 2.8 copy-start.7
  236.8 3.7 %copy-start.4 = (f32[1,320,2432]{2,1,0:T(8,128)S(1)}, f32[1,320,2432]{2,1,0:T(8,128)}, u32[]{:S(2)}) copy-start(f32[1,320,2432]{2,1,0:T(8,128)} %copy-done.3) | copy-start | bytes 9338884
  236.8 4.2 %copy-start.8 = (bf16[1,2,320,2432]{3,2,1,0:T(8,128)(2,1)S(1)}, bf16[1,2,320,2432]{3,2,1,0:T(8,128)(2,1)}, u32[]{:S(2)}) copy-start(bf16[1,2,320,2432]{3,2,1,0:T(8,128)(2,1)} %param.11) | copy-start | bytes 9338884
  236.8 13.8 %slice-start.2 = ((s8[6225920]{0:T(1024)(128)(4,1)}), s8[4194304]{0:T(1024)(128)(4,1)S(1)}, s32[]{:S(2)}) async-start(s8[6225920]{0:T(1024)(128)(4,1)} %bitcast.183), calls=%async_computation.4 | async-start | bytes 8388608
  241.0 3.5 copy-start.9
  241.1 9.6 %slice-start.3 = ((s8[6225920]{0:T(1024)(128)(4,1)}), s8[2031616]{0:T(1024)(128)(4,1)S(1)}, s32[]{:S(2)}) async-start(s8[6225920]{0:T(1024)(128)(4,1)} %bitcast.183), calls=%async_computation.5 | async-start | bytes 4063232
  244.5 6.1 %copy-start.15 = (f32[320,1216]{1,0:T(8,128)S(1)}, f32[320,1216]{1,0:T(8,128)}, u32[]{:S(2)}) copy-start(f32[320,1216]{1,0:T(8,128)} %copy-done.14) | copy-start | bytes 4669444
  250.6 2.9 copy-start.13
  253.6 2.9 copy-start.10
  253.6 2.9 copy-start.11
  356.4 2.8 copy-start.16
  356.4 3.9 %copy-start.1 = (f32[10,2,2432]{2,1,0:T(2,128)S(1)}, f32[10,2,2432]{2,1,0:T(2,128)}, u32[]{:S(2)}) copy-start(f32[10,2,2432]{2,1,0:T(2,128)} %param.15) | copy-start | bytes 583684
Sparse Core Ops, SparseCore 0:
  9.6 48.6 all-gather.2
  59.9 45.9 all-gather.4
